TPU v7x, 32 devices: a whole 2x2x4 slice. The times are simulated.
32 devices in a mesh: dp: 8 (over y, x, core), mp: 4 (over z).
Axes of the slice: x: 2, y: 2, z: 4, core: 2. Of those that a mesh axis runs over, the one named last changes fastest.
Arguments:
- tokens: bfloat16 [16384, 512], P(('dp', 'mp')), may hold values from -6 to 6
- doc_ids: int32 [16, 1024], P('dp'), may hold values from 0 to 7, never falling along the last dimension, each value on 1 to 512 neighbouring positions
- resets: int32 [16], P('dp'), may hold values from 1 to 1023
- norm_one_gain: float32 [512], replicated, may hold values from 0.1 to 1.9
- norm_one_bias: float32 [512], replicated, may hold values from -3 to 3
- query_weight: bfloat16 [512, 512], P(None, 'mp'), may hold values from -0.25 to 0.25
- key_weight: bfloat16 [512, 512], P(None, 'mp'), may hold values from -0.25 to 0.25
- value_weight: bfloat16 [512, 512], P(None, 'mp'), may hold values from -0.25 to 0.25
- output_weight: bfloat16 [512, 512], P('mp'), may hold values from -2 to 2
- output_bias: float32 [512], replicated, may hold values from -3 to 3
- gate_one_weight: bfloat16 [512, 512], replicated, may hold values from -0.25 to 0.25
- gate_one_bias: float32 [512], replicated, may hold values from -3 to 3
- norm_two_gain: float32 [512], replicated, may hold values from 0.1 to 1.9
- norm_two_bias: float32 [512], replicated, may hold values from -3 to 3
- up_weight: bfloat16 [512, 2048], P(None, 'mp'), may hold values from -0.25 to 0.25
- up_bias: float32 [2048], P('mp'), may hold values from -3 to 3
- down_weight: bfloat16 [2048, 512], P('mp'), may hold values from -0.25 to 0.25
- down_bias: float32 [512], replicated, may hold values from -3 to 3
- gate_two_weight: bfloat16 [512, 512], replicated, may hold values from -0.25 to 0.25
- gate_two_bias: float32 [512], replicated, may hold values from -3 to 3
- cotangent: bfloat16 [16384, 512], P(('dp', 'mp')), may hold values from -6 to 6
Outputs:
- output: bfloat16 [16384, 512], P(('dp', 'mp'))
- grad_tokens: float32 [16384, 512], P(('dp', 'mp'))
- grad_norm_one_gain: float32 [512], replicated
- grad_norm_one_bias: float32 [512], replicated
- grad_query_weight: float32 [512, 512], P(None, 'mp')
- grad_key_weight: float32 [512, 512], P(None, 'mp')
- grad_value_weight: float32 [512, 512], P(None, 'mp')
- grad_output_weight: float32 [512, 512], P('mp')
- grad_output_bias: float32 [512], replicated
- grad_gate_one_weight: float32 [512, 512], replicated
- grad_gate_one_bias: float32 [512], replicated
- grad_norm_two_gain: float32 [512], replicated
- grad_norm_two_bias: float32 [512], replicated
- grad_up_weight: float32 [512, 2048], P(None, 'mp')
- grad_up_bias: float32 [2048], P('mp')
- grad_down_weight: float32 [2048, 512], P('mp')
- grad_down_bias: float32 [512], replicated
- grad_gate_two_weight: float32 [512, 512], replicated
- grad_gate_two_bias: float32 [512], replicated
Inputs may be any that keep to these rules, and one draw needn't show every extreme that they name: `doc_ids`: within a row the ids never fall, and each id covers 1 to 512 tokens of the row.
All inputs are finite; a program needn't handle non-finite values.
Results may differ from a plain program's by a relative error of at most 0.018.
Values may be sent and summed in bfloat16 or wider, within the bound.
A program may use at most 128 MiB of HBM per device.

v0:
```python
import math

import jax
import jax.numpy as jnp
from jax import lax
from jax.sharding import PartitionSpec as P

HDIM = 64


def layer_norm(values, gain, bias):
    centered = values - jnp.mean(values, axis=-1, keepdims=True)
    variance = jnp.mean(centered * centered, axis=-1, keepdims=True)
    return centered * lax.rsqrt(variance + 1e-05) * gain + bias


def rotary_tables(resets, seq_len):
    steps = jnp.arange(seq_len, dtype=jnp.int32)
    places = jnp.where(
        steps[None, :] >= resets[:, None], steps[None, :] - resets[:, None], steps[None, :]
    )
    freqs = jnp.exp(jnp.arange(HDIM // 2, dtype=jnp.float32) * (-2.0 * math.log(10000.0) / HDIM))
    angles = places.astype(jnp.float32)[:, :, None] * freqs
    return (jnp.cos(angles)[:, :, None, :], jnp.sin(angles)[:, :, None, :])


def rotate(values, cosine, sine):
    first, second = jnp.split(values, 2, axis=-1)
    return jnp.concatenate(
        [first * cosine - second * sine, second * cosine + first * sine], axis=-1
    )


def rotate_back(grads, cosine, sine):
    first, second = jnp.split(grads, 2, axis=-1)
    return jnp.concatenate(
        [first * cosine + second * sine, second * cosine - first * sine], axis=-1
    )


def contract_rows(left, right):
    return lax.dot_general(
        left, right, (((0,), (0,)), ((), ())), preferred_element_type=jnp.float32
    )


def contract_cols(left, right):
    return lax.dot_general(
        left, right, (((1,), (1,)), ((), ())), preferred_element_type=jnp.float32
    )


def masked_scores(query, keys, docs):
    scale = 1.0 / math.sqrt(HDIM)
    scores = jnp.einsum("qhd,khd->hqk", query, keys, preferred_element_type=jnp.float32) * scale
    places = jnp.arange(docs.shape[0], dtype=jnp.int32)
    allowed = (docs[:, None] == docs[None, :]) & (places[None, :] <= places[:, None])
    return jnp.where(allowed[None], scores, -1e30)


def attend_forward(bundle):
    query, keys, values, docs = bundle
    scores = masked_scores(query, keys, docs)
    highest = jnp.max(scores, axis=-1, keepdims=True)
    weights = jnp.exp(scores - highest)
    total = jnp.sum(weights, axis=-1, keepdims=True)
    probs = (weights / total).astype(jnp.bfloat16)
    context = jnp.einsum("hqk,khd->qhd", probs, values, preferred_element_type=jnp.float32)
    return (context.astype(jnp.bfloat16), (highest + jnp.log(total))[..., 0])


def attend_backward(bundle):
    query, keys, values, docs, logsum, grad_context = bundle
    scale = 1.0 / math.sqrt(HDIM)
    probs = jnp.exp(masked_scores(query, keys, docs) - logsum[..., None])
    rounded = probs.astype(jnp.bfloat16)
    grad_values = jnp.einsum(
        "hqk,qhd->khd", rounded, grad_context, preferred_element_type=jnp.float32
    )
    grad_probs = jnp.einsum(
        "qhd,khd->hqk", grad_context, values, preferred_element_type=jnp.float32
    )
    inner = jnp.sum(grad_probs * probs, axis=-1, keepdims=True)
    grad_scores = (probs * (grad_probs - inner)).astype(jnp.bfloat16)
    grad_query = (
        jnp.einsum("hqk,khd->qhd", grad_scores, keys, preferred_element_type=jnp.float32) * scale
    )
    grad_keys = (
        jnp.einsum("hqk,qhd->khd", grad_scores, query, preferred_element_type=jnp.float32) * scale
    )
    return (grad_query, grad_keys, grad_values)


def shards(
    tokens,
    doc_ids,
    resets,
    norm_one_gain,
    norm_one_bias,
    query_weight,
    key_weight,
    value_weight,
    output_weight,
    output_bias,
    gate_one_weight,
    gate_one_bias,
    norm_two_gain,
    norm_two_bias,
    up_weight,
    up_bias,
    down_weight,
    down_bias,
    gate_two_weight,
    gate_two_bias,
    cotangent,
):
    row_count, seq_len = doc_ids.shape
    head_width = query_weight.shape[1]
    heads_here = head_width // HDIM
    grid = (row_count, seq_len, heads_here, HDIM)
    inputs = tokens.astype(jnp.float32)
    cosine, sine = rotary_tables(resets, seq_len)
    joined_weight = jnp.concatenate([query_weight, key_weight, value_weight], axis=1)
    normed_one = layer_norm(inputs, norm_one_gain, norm_one_bias)
    rounded_one = normed_one.astype(jnp.bfloat16)
    rows_one = lax.all_gather(rounded_one, "mp", axis=0, tiled=True)
    projected = jnp.dot(rows_one, joined_weight, preferred_element_type=jnp.float32)
    query = rotate(projected[:, :head_width].reshape(grid), cosine, sine).astype(jnp.bfloat16)
    keys = rotate(projected[:, head_width : 2 * head_width].reshape(grid), cosine, sine).astype(
        jnp.bfloat16
    )
    values = projected[:, 2 * head_width :].reshape(grid).astype(jnp.bfloat16)
    context, logsum = lax.map(attend_forward, (query, keys, values, doc_ids))
    context = context.reshape(row_count * seq_len, head_width)
    attended = (
        lax.psum_scatter(
            jnp.dot(context, output_weight, preferred_element_type=jnp.float32),
            "mp",
            scatter_dimension=0,
            tiled=True,
        )
        + output_bias
    )
    gate_one = jax.nn.sigmoid(
        jnp.dot(rounded_one, gate_one_weight, preferred_element_type=jnp.float32) + gate_one_bias
    )
    middle = inputs + gate_one * (attended - inputs)
    normed_two = layer_norm(middle, norm_two_gain, norm_two_bias)
    rounded_two = normed_two.astype(jnp.bfloat16)
    rows_two = lax.all_gather(rounded_two, "mp", axis=0, tiled=True)
    pre_act = jnp.dot(rows_two, up_weight, preferred_element_type=jnp.float32) + up_bias
    hidden = jax.nn.gelu(pre_act, approximate=True).astype(jnp.bfloat16)
    branch = (
        lax.psum_scatter(
            jnp.dot(hidden, down_weight, preferred_element_type=jnp.float32).astype(jnp.bfloat16),
            "mp",
            scatter_dimension=0,
            tiled=True,
        ).astype(jnp.float32)
        + down_bias
    )
    gate_two = jax.nn.sigmoid(
        jnp.dot(rounded_two, gate_two_weight, preferred_element_type=jnp.float32) + gate_two_bias
    )
    output = middle + gate_two * (branch - middle)
    grad_out = cotangent.astype(jnp.float32)
    grad_branch = gate_two * grad_out
    grad_down_bias = jnp.sum(grad_branch, axis=0)
    grad_gate_two = grad_out * (branch - middle) * gate_two * (1.0 - gate_two)
    grad_gate_two_bias = jnp.sum(grad_gate_two, axis=0)
    gate_two_low = grad_gate_two.astype(jnp.bfloat16)
    grad_gate_two_weight = contract_rows(rounded_two, gate_two_low)
    rows_branch = lax.all_gather(grad_branch.astype(jnp.bfloat16), "mp", axis=0, tiled=True)
    grad_hidden = contract_cols(rows_branch, down_weight)
    grad_down_weight = contract_rows(hidden, rows_branch)
    gelu_value, gelu_back = jax.vjp(
        lambda activation: jax.nn.gelu(activation, approximate=True), pre_act
    )
    grad_pre = gelu_back(grad_hidden)[0]
    grad_up_bias = jnp.sum(grad_pre, axis=0)
    pre_low = grad_pre.astype(jnp.bfloat16)
    grad_up_weight = contract_rows(rows_two, pre_low)
    grad_normed_two = lax.psum_scatter(
        contract_cols(pre_low, up_weight).astype(jnp.bfloat16),
        "mp",
        scatter_dimension=0,
        tiled=True,
    ).astype(jnp.float32)
    grad_normed_two = grad_normed_two + contract_cols(gate_two_low, gate_two_weight)
    norm_value, norm_two_back = jax.vjp(layer_norm, middle, norm_two_gain, norm_two_bias)
    grad_middle, grad_norm_two_gain, grad_norm_two_bias = norm_two_back(grad_normed_two)
    grad_middle = grad_middle + grad_out * (1.0 - gate_two)
    grad_attended = gate_one * grad_middle
    grad_output_bias = jnp.sum(grad_attended, axis=0)
    grad_gate_one = grad_middle * (attended - inputs) * gate_one * (1.0 - gate_one)
    grad_gate_one_bias = jnp.sum(grad_gate_one, axis=0)
    gate_one_low = grad_gate_one.astype(jnp.bfloat16)
    grad_gate_one_weight = contract_rows(rounded_one, gate_one_low)
    rows_attended = lax.all_gather(grad_attended.astype(jnp.bfloat16), "mp", axis=0, tiled=True)
    grad_context = contract_cols(rows_attended, output_weight).astype(jnp.bfloat16)
    grad_output_weight = contract_rows(context, rows_attended)
    grad_query, grad_keys, grad_values = lax.map(
        attend_backward, (query, keys, values, doc_ids, logsum, grad_context.reshape(grid))
    )
    grad_query = rotate_back(grad_query, cosine, sine).reshape(row_count * seq_len, head_width)
    grad_keys = rotate_back(grad_keys, cosine, sine).reshape(row_count * seq_len, head_width)
    grad_values = grad_values.reshape(row_count * seq_len, head_width)
    grad_joined = jnp.concatenate([grad_query, grad_keys, grad_values], axis=1).astype(jnp.bfloat16)
    grad_joined_weight = contract_rows(rows_one, grad_joined)
    grad_normed_one = lax.psum_scatter(
        contract_cols(grad_joined, joined_weight).astype(jnp.bfloat16),
        "mp",
        scatter_dimension=0,
        tiled=True,
    ).astype(jnp.float32)
    grad_normed_one = grad_normed_one + contract_cols(gate_one_low, gate_one_weight)
    first_value, norm_one_back = jax.vjp(layer_norm, inputs, norm_one_gain, norm_one_bias)
    grad_inputs, grad_norm_one_gain, grad_norm_one_bias = norm_one_back(grad_normed_one)
    grad_inputs = grad_inputs + grad_middle * (1.0 - gate_one)
    grad_joined_weight, grad_output_weight, grad_up_weight, grad_up_bias, grad_down_weight = (
        lax.psum(
            (
                grad_joined_weight,
                grad_output_weight,
                grad_up_weight,
                grad_up_bias,
                grad_down_weight,
            ),
            "dp",
        )
    )
    (
        grad_gate_one_weight,
        grad_gate_one_bias,
        grad_output_bias,
        grad_norm_one_gain,
        grad_norm_one_bias,
        grad_gate_two_weight,
        grad_gate_two_bias,
        grad_down_bias,
        grad_norm_two_gain,
        grad_norm_two_bias,
    ) = lax.psum(
        (
            grad_gate_one_weight,
            grad_gate_one_bias,
            grad_output_bias,
            grad_norm_one_gain,
            grad_norm_one_bias,
            grad_gate_two_weight,
            grad_gate_two_bias,
            grad_down_bias,
            grad_norm_two_gain,
            grad_norm_two_bias,
        ),
        ("dp", "mp"),
    )
    grad_query_weight = grad_joined_weight[:, :head_width]
    grad_key_weight = grad_joined_weight[:, head_width : 2 * head_width]
    grad_value_weight = grad_joined_weight[:, 2 * head_width :]
    return (
        output.astype(jnp.bfloat16),
        grad_inputs,
        grad_norm_one_gain,
        grad_norm_one_bias,
        grad_query_weight,
        grad_key_weight,
        grad_value_weight,
        grad_output_weight,
        grad_output_bias,
        grad_gate_one_weight,
        grad_gate_one_bias,
        grad_norm_two_gain,
        grad_norm_two_bias,
        grad_up_weight,
        grad_up_bias,
        grad_down_weight,
        grad_down_bias,
        grad_gate_two_weight,
        grad_gate_two_bias,
    )


def solution(mesh):
    in_specs = (
        P(("dp", "mp"), None),
        P("dp", None),
        P("dp"),
        P(),
        P(),
        P(None, "mp"),
        P(None, "mp"),
        P(None, "mp"),
        P("mp", None),
        P(),
        P(),
        P(),
        P(),
        P(),
        P(None, "mp"),
        P("mp"),
        P("mp", None),
        P(),
        P(),
        P(),
        P(("dp", "mp"), None),
    )
    out_specs = (
        P(("dp", "mp"), None),
        P(("dp", "mp"), None),
        P(),
        P(),
        P(None, "mp"),
        P(None, "mp"),
        P(None, "mp"),
        P("mp", None),
        P(),
        P(),
        P(),
        P(),
        P(),
        P(None, "mp"),
        P("mp"),
        P("mp", None),
        P(),
        P(),
        P(),
    )
    return jax.shard_map(shards, mesh=mesh, in_specs=in_specs, out_specs=out_specs, check_vma=False)
```

profile of v0, /device:TPU:0, one launch (start us, length us, event | category | flops | bytes accessed | tf_op | source)
XLA Modules:
  0.0 781.6 jit_solution(10302197833076697984)
XLA Ops:
  9.9 2.1 fusion.75
  15.7 4.0 multiply_cosine_fusion
  19.7 41.1 %all-gather.5.cloned.1.call-done = bf16[2048,512]{1,0:T(8,128)(2,1)} async-done(((bf16[512,512]{1,0:T(8,128)(2,1)}), bf16[2048,512]{1,0:T(8,128)(2,1)}) %all-gather.5.cloned.1.call-update) | async-done | bytes 2097168 | tf_op jit(solution)/shard_map/all_gather | solution.py:126
  60.7 2.8 fusion.110
  66.8 2.5 reshape.310
  71.1 2.5 copy.56
  78.6 17.1 %while.26 = (s32[]{:T(128)}, bf16[2,1024,2,64]{1,3,2,0:T(8,128)(2,1)S(1)}, f32[2,2,1024]{2,1,0:T(2,128)S(1)}, bf16[2,1024,2,64]{1,3,2,0:T(8,128)(2,1)}, s32[2,10...) while((s32[]{:T(128)}, ...), condition=%wide.region_5.6_spmd, body=%wide.region_2.5_spmd.sunk | while | flops 565311488 | bytes 30488676 | solution.py:133
  83.6 3.8 fusion.174
  91.9 3.8 fusion.174
  97.2 2.7 fusion.111
  100.0 75.7 %reduce-scatter.5.cloned.1.call-done = f32[512,512]{1,0:T(8,128)} async-done(((f32[2048,512]{1,0:T(8,128)}), f32[512,512]{1,0:T(8,128)}) %reduce-scatter.5.cloned.1.call-update) | async-done | bytes 1048592 | tf_op jit(solution)/shard_map/reduce_scatter | solution.py:136
  175.8 2.9 fusion.105
  180.9 2.9 fusion.86
  183.9 43.5 %all-gather.7.cloned.1.call-done = bf16[2048,512]{1,0:T(8,128)(2,1)} async-done(((bf16[512,512]{1,0:T(8,128)(2,1)}), bf16[2048,512]{1,0:T(8,128)(2,1)}) %all-gather.7.cloned.1.call-update) | async-done | bytes 2097168 | tf_op jit(solution)/shard_map/all_gather | solution.py:150
  227.4 4.8 fusion.112
  232.2 42.0 %all-gather.9.cloned.1.call-done = bf16[2048,512]{1,0:T(8,128)(2,1)} async-done(((bf16[512,512]{1,0:T(8,128)(2,1)}), bf16[2048,512]{1,0:T(8,128)(2,1)}) %all-gather.9.cloned.1.call-update) | async-done | bytes 2097168 | tf_op jit(solution)/shard_map/all_gather | solution.py:173
  274.2 7.1 fusion.98
  282.6 2.6 convolution_convert_fusion.2
  285.4 4.4 convolution_convert_fusion.1
  289.8 38.0 %reduce-scatter.7.cloned.1.call-done = bf16[512,512]{1,0:T(8,128)(2,1)} async-done(((bf16[2048,512]{1,0:T(8,128)(2,1)}), bf16[512,512]{1,0:T(8,128)(2,1)}) %reduce-scatter.7.cloned.1.call-update) | async-done | bytes 524304 | tf_op jit(solution)/shard_map/reduce_scatter | solution.py:154
  327.9 2.7 fusion.100
  330.6 42.7 %reduce-scatter.9.cloned.1.call-done = bf16[512,512]{1,0:T(8,128)(2,1)} async-done(((bf16[2048,512]{1,0:T(8,128)(2,1)}), bf16[512,512]{1,0:T(8,128)(2,1)}) %reduce-scatter.9.cloned.1.call-update) | async-done | bytes 524304 | tf_op jit(solution)/shard_map/reduce_scatter | solution.py:183
  373.3 2.1 multiply_reduce_fusion.1
  379.3 4.7 fusion.115
  384.0 2.2 fusion.82
  386.3 38.4 %all-gather.11.cloned.1.call-done = bf16[2048,512]{1,0:T(8,128)(2,1)} async-done(((bf16[512,512]{1,0:T(8,128)(2,1)}), bf16[2048,512]{1,0:T(8,128)(2,1)}) %all-gather.11.cloned.1.call-update) | async-done | bytes 2097168 | tf_op jit(solution)/shard_map/all_gather | solution.py:199
  424.6 2.3 convolution_convert_fusion.3
  429.2 72.6 %while.27 = (s32[]{:T(128)}, f32[2,1024,2,64]{1,0,3,2:T(2,128)}, f32[2,1024,2,64]{1,0,3,2:T(2,128)}, bf16[2,1024,2,64]{1,3,2,0:T(8,128)(2,1)}, bf16[2,1024,2,64]...) while((s32[]{:T(128)}, f32[2,1024,2,64]{1,0,3,2:T(2,128)}, ...), condition=%wide.region_15.16_spmd, body=%wide.region_13.15_spmd.sunk | while | flops 1377040384 | bytes 74783896 | solution.py:202
  431.2 4.2 fusion.187
  435.4 4.2 multiply_reduce_fusion.6
  439.5 2.7 multiply_convert_fusion.4
  445.6 10.0 %dynamic_update_slice.30 = f32[2,1024,2,64]{1,0,3,2:T(2,128)} dynamic-update-slice(f32[2,1024,2,64]{1,0,3,2:T(2,128)} %get-tuple-element.411, f32[1,1024,2,64]{1,0,3,2:T(1,128)S(1)} %copy.108, s32[]{:T(128)S(6)} %copy.129, s32[]{:T(128)} %constant.74.clone.1..sunk, s32[]{:T(128)} %constant.74.clone.1..sunk, s32[]{:T(128)} %constant.74.clone.1..sunk) | dynamic-update-slice | bytes 1048580 | tf_op jit(solution)/shard_map/while/body/jit(dynamic_update_index_in_dim)/dynamic_update_slice | solution.py:202
  455.6 10.0 %dynamic_update_slice.29 = f32[2,1024,2,64]{1,0,3,2:T(2,128)} dynamic-update-slice(f32[2,1024,2,64]{1,0,3,2:T(2,128)} %get-tuple-element.410, f32[1,1024,2,64]{1,0,3,2:T(1,128)S(1)} %copy.107, s32[]{:T(128)S(6)} %copy.129, s32[]{:T(128)} %constant.74.clone.1..sunk, s32[]{:T(128)} %constant.74.clone.1..sunk, s32[]{:T(128)} %constant.74.clone.1..sunk) | dynamic-update-slice | bytes 1048580 | tf_op jit(solution)/shard_map/while/body/jit(dynamic_update_index_in_dim)/dynamic_update_slice | solution.py:202
  467.5 4.2 fusion.187
  471.7 4.2 multiply_reduce_fusion.6
  475.8 2.7 multiply_convert_fusion.4
  481.9 10.0 %dynamic_update_slice.30 = f32[2,1024,2,64]{1,0,3,2:T(2,128)} dynamic-update-slice(f32[2,1024,2,64]{1,0,3,2:T(2,128)} %get-tuple-element.411, f32[1,1024,2,64]{1,0,3,2:T(1,128)S(1)} %copy.108, s32[]{:T(128)S(6)} %copy.129, s32[]{:T(128)} %constant.74.clone.1..sunk, s32[]{:T(128)} %constant.74.clone.1..sunk, s32[]{:T(128)} %constant.74.clone.1..sunk) | dynamic-update-slice | bytes 1048580 | tf_op jit(solution)/shard_map/while/body/jit(dynamic_update_index_in_dim)/dynamic_update_slice | solution.py:202
  491.9 10.0 %dynamic_update_slice.29 = f32[2,1024,2,64]{1,0,3,2:T(2,128)} dynamic-update-slice(f32[2,1024,2,64]{1,0,3,2:T(2,128)} %get-tuple-element.410, f32[1,1024,2,64]{1,0,3,2:T(1,128)S(1)} %copy.107, s32[]{:T(128)S(6)} %copy.129, s32[]{:T(128)} %constant.74.clone.1..sunk, s32[]{:T(128)} %constant.74.clone.1..sunk, s32[]{:T(128)} %constant.74.clone.1..sunk) | dynamic-update-slice | bytes 1048580 | tf_op jit(solution)/shard_map/while/body/jit(dynamic_update_index_in_dim)/dynamic_update_slice | solution.py:202
  503.6 2.6 add_convert_fusion.2
  509.2 2.3 fusion.113
  511.7 4.1 convolution_convert_fusion
  515.9 14.9 %psum.115 = f32[512]{0:T(512)} all-reduce(f32[512]{0:T(512)S(1)} %get-tuple-element.205), channel_id=1, replica_groups=mesh['dp'=8,'mp'=4] {'dp'}, use_global_device_ids=true, to_apply=%region_36.37 | all-reduce | flops 512 | bytes 4096 | tf_op jit(solution)/shard_map/psum | solution.py:221
  533.9 46.8 %all-reduce.8.cloned.1.call-done = (f32[512,384]{1,0:T(8,128)}, f32[128,512]{1,0:T(8,128)}, f32[512,512]{1,0:T(8,128)}, f32[512,512]{1,0:T(8,128)}) async-done(((f32[512,384]{1,0:T(8,128)}, f32[128,512]{1,0:T(8,128)}, f32[512,512]{1,0:T(8,128)}, f32[512,512]{1,0:T(8,128)}), (f32[512,384]{1,0:T(8,128)}, f32[128,512]{1,0:T(8,128)}, f32[512,512]{1,0:T(8,128)}, ...) | async-done | bytes 3145744 | tf_op jit(solution)/shard_map/psum | solution.py:221
  582.7 44.3 %reduce-scatter.11.cloned.1.call-done = bf16[512,512]{1,0:T(8,128)(2,1)} async-done(((bf16[2048,512]{1,0:T(8,128)(2,1)}), bf16[512,512]{1,0:T(8,128)(2,1)}) %reduce-scatter.11.cloned.1.call-update) | async-done | bytes 524304 | tf_op jit(solution)/shard_map/reduce_scatter | solution.py:210
  631.0 39.9 %all-reduce = (f32[512]{0:T(512)}, f32[512]{0:T(512)}, f32[512]{0:T(512)}, f32[512]{0:T(512)}, f32[512]{0:T(512)}, /*index=5*/f32[512]{0:T(512)}, f32[512]{0:T(512)}, f32[512]{0:T(512)}) all-reduce(f32[512]{0:T(512)S(1)} %get-tuple-element.152, f32[512]{0:T(512)S(1)} %get-tuple-element.155, ...), channel_id=1, replica_groups=mesh['dp'=8,'mp'=4] {'dp','mp'}, use_global_device_ids=true, to_apply=%region_20.21 | all-reduce | flops 4096 | bytes 32768 | tf_op jit(solution)/shard_map/psum | solution.py:243
  670.9 96.4 %all-reduce.6.cloned.1.call-done = (f32[512,512]{1,0:T(8,128)}, f32[512,512]{1,0:T(8,128)}) async-done(((f32[512,512]{1,0:T(8,128)}, f32[512,512]{1,0:T(8,128)}), (f32[512,512]{1,0:T(8,128)}, f32[512,512]{1,0:T(8,128)})) %all-reduce.6.cloned.1.call-update) | async-done | bytes 2097168 | tf_op jit(solution)/shard_map/psum | solution.py:243
  768.0 2.3 copy.146
  770.3 2.3 copy.147
  (216 shorter events, 63.7 us)
Async XLA Ops:
  7.2 267.0 %copy-start = (bf16[512,512]{1,0:T(8,128)(2,1)S(1)}, bf16[512,512]{1,0:T(8,128)(2,1)}, u32[]{:S(2)}) copy-start(bf16[512,512]{1,0:T(8,128)(2,1)} %param.41) | copy-start | bytes 1572868
  7.2 53.5 %all-gather.5.cloned.1.call-start = ((), (), s32[]{:S(2)}) async-start(), calls=%async_computation.4 | async-start | bytes 2621440 | tf_op jit(solution)/shard_map/all_gather | solution.py:126
  8.5 167.3 %copy-start.36 = (f32[512]{0:T(512)}, f32[512]{0:T(512)S(1)}, u32[]{:S(2)}) copy-start(f32[512]{0:T(512)S(1)} %broadcast_multiply_fusion.1) | copy-start | bytes 6148
  9.9 165.9 %copy-start.38 = (f32[512]{0:T(512)}, f32[512]{0:T(512)S(1)}, u32[]{:S(2)}) copy-start(f32[512]{0:T(512)S(1)} %fusion.94) | copy-start | bytes 6148
  12.0 163.8 %reduce-scatter.5.cloned.1.call-start = ((), (), s32[]{:S(2)}) async-start(), calls=%async_computation.5 | async-start | bytes 5242880 | tf_op jit(solution)/shard_map/reduce_scatter | solution.py:136
  14.9 48.7 %copy-start.26 = (bf16[512,384]{1,0:T(8,128)(2,1)}, bf16[512,384]{1,0:T(8,128)(2,1)S(1)}, u32[]{:S(2)}) copy-start(bf16[512,384]{1,0:T(8,128)(2,1)S(1)} %constant_dynamic-update-slice_fusion) | copy-start | bytes 1179652
  19.7 56.1 %copy-start.16 = (f32[2,1024,32]{1,0,2:T(2,128)}, f32[2,1024,32]{1,0,2:T(2,128)S(1)}, u32[]{:S(2)}) copy-start(f32[2,1024,32]{1,0,2:T(2,128)S(1)} %get-tuple-element.242) | copy-start | bytes 786436
  19.7 56.1 %copy-start.18 = (f32[2,1024,32]{1,0,2:T(2,128)}, f32[2,1024,32]{1,0,2:T(2,128)S(1)}, u32[]{:S(2)}) copy-start(f32[2,1024,32]{1,0,2:T(2,128)S(1)} %get-tuple-element.243) | copy-start | bytes 786436
  78.6 18.6 %copy-start.32 = (bf16[128,512]{1,0:T(8,128)(2,1)S(1)}, bf16[128,512]{1,0:T(8,128)(2,1)}, u32[]{:S(2)}) copy-start(bf16[128,512]{1,0:T(8,128)(2,1)} %param.33) | copy-start | bytes 393220
  97.2 78.6 %copy-start.2 = (bf16[512,512]{1,0:T(8,128)(2,1)S(1)}, bf16[512,512]{1,0:T(8,128)(2,1)}, u32[]{:S(2)}) copy-start(bf16[512,512]{1,0:T(8,128)(2,1)} %param.25) | copy-start | bytes 1572868
  97.2 78.6 %copy-start.40 = (f32[512]{0:T(512)S(1)}, f32[512]{0:T(512)}, u32[]{:S(2)}) copy-start(f32[512]{0:T(512)} %param.28) | copy-start | bytes 6148
  97.2 78.6 %copy-start.47 = (f32[512]{0:T(512)S(1)}, f32[512]{0:T(512)}, u32[]{:S(2)}) copy-start(f32[512]{0:T(512)} %param.34) | copy-start | bytes 6148
  97.2 78.6 %copy-start.48 = (f32[512]{0:T(512)S(1)}, f32[512]{0:T(512)}, u32[]{:S(2)}) copy-start(f32[512]{0:T(512)} %param.29) | copy-start | bytes 6148
  97.2 78.6 %copy-start.50 = (bf16[512,512]{1,0:T(8,128)(2,1)S(1)}, bf16[512,512]{1,0:T(8,128)(2,1)}, u32[]{:S(2)}) copy-start(bf16[512,512]{1,0:T(8,128)(2,1)} %param.35) | copy-start | bytes 1572868
  97.2 78.6 %copy-start.51 = (f32[512]{0:T(512)S(1)}, f32[512]{0:T(512)}, u32[]{:S(2)}) copy-start(f32[512]{0:T(512)} %param.36) | copy-start | bytes 6148
  99.9 79.8 %copy-start.44 = (f32[512]{0:T(512)S(1)}, f32[512]{0:T(512)}, u32[]{:S(2)}) copy-start(f32[512]{0:T(512)} %param.37) | copy-start | bytes 6148
  99.9 79.8 %copy-start.46 = (f32[512]{0:T(512)S(1)}, f32[512]{0:T(512)}, u32[]{:S(2)}) copy-start(f32[512]{0:T(512)} %param.38) | copy-start | bytes 6148
  100.0 80.9 %copy-start.21 = (bf16[512,512]{1,0:T(8,128)(2,1)S(1)}, bf16[512,512]{1,0:T(8,128)(2,1)}, u32[]{:S(2)}) copy-start(bf16[512,512]{1,0:T(8,128)(2,1)} %param.45) | copy-start | bytes 1572868
  100.0 80.9 %copy-start.52 = (f32[512]{0:T(512)S(1)}, f32[512]{0:T(512)}, u32[]{:S(2)}) copy-start(f32[512]{0:T(512)} %param.44) | copy-start | bytes 6148
  100.0 127.4 %all-gather.7.cloned.1.call-start = ((), (), s32[]{:S(2)}) async-start(), calls=%async_computation.6 | async-start | bytes 2621440 | tf_op jit(solution)/shard_map/all_gather | solution.py:150
  179.7 47.7 %copy-start.28 = (bf16[512,512]{1,0:T(8,128)(2,1)S(1)}, bf16[512,512]{1,0:T(8,128)(2,1)}, u32[]{:S(2)}) copy-start(bf16[512,512]{1,0:T(8,128)(2,1)} %param.39) | copy-start | bytes 1572868
  180.8 93.4 %all-gather.9.cloned.1.call-start = ((), (), s32[]{:S(2)}) async-start(), calls=%async_computation.8 | async-start | bytes 2621440 | tf_op jit(solution)/shard_map/all_gather | solution.py:173
  183.8 90.3 %copy-start.53 = (f32[512]{0:T(512)S(1)}, f32[512]{0:T(512)}, u32[]{:S(2)}) copy-start(f32[512]{0:T(512)} %param.40) | copy-start | bytes 6148
  183.8 144.0 %reduce-scatter.7.cloned.1.call-start = ((), (), s32[]{:S(2)}) async-start(), calls=%async_computation.7 | async-start | bytes 2621440 | tf_op jit(solution)/shard_map/reduce_scatter | solution.py:154
  285.1 88.1 %reduce-scatter.9.cloned.1.call-start = ((), (), s32[]{:S(2)}) async-start(), calls=%async_computation.9 | async-start | bytes 2621440 | tf_op jit(solution)/shard_map/reduce_scatter | solution.py:183
  285.4 42.5 %copy-start.4 = (f32[512,512]{1,0:T(8,128)S(1)}, f32[512,512]{1,0:T(8,128)}, u32[]{:S(2)}) copy-start(f32[512,512]{1,0:T(8,128)} %copy-done.3) | copy-start | bytes 3145732
  285.4 42.5 %copy-start.45 = (f32[512]{0:T(512)S(1)}, f32[512]{0:T(512)}, u32[]{:S(2)}) copy-start(f32[512]{0:T(512)} %param.42) | copy-start | bytes 6148
  289.8 134.9 %all-gather.11.cloned.1.call-start = ((), (), s32[]{:S(2)}) async-start(), calls=%async_computation.10 | async-start | bytes 2621440 | tf_op jit(solution)/shard_map/all_gather | solution.py:199
  330.6 46.7 %copy-start.19 = (bf16[512,512]{1,0:T(8,128)(2,1)}, bf16[512,512]{1,0:T(8,128)(2,1)S(1)}, u32[]{:S(2)}) copy-start(bf16[512,512]{1,0:T(8,128)(2,1)S(1)} %get-tuple-element.208) | copy-start | bytes 1572868
  379.2 201.5 %all-reduce.8.cloned.1.call-start = ((), (), s32[]{:S(2)}) async-start(), calls=%async_computation.13 | async-start | bytes 6291456 | tf_op jit(solution)/shard_map/psum | solution.py:221
  429.2 74.3 %copy-start.17 = (f32[2,1024,32]{1,0,2:T(2,128)S(1)}, f32[2,1024,32]{1,0,2:T(2,128)}, u32[]{:S(2)}) copy-start(f32[2,1024,32]{1,0,2:T(2,128)} %copy-done.16) | copy-start | bytes 786436
  511.5 19.2 %copy-start.10 = (bf16[512,512]{1,0:T(8,128)(2,1)S(1)}, bf16[512,512]{1,0:T(8,128)(2,1)}, u32[]{:S(2)}) copy-start(bf16[512,512]{1,0:T(8,128)(2,1)} %add_convert_fusion.1) | copy-start | bytes 1572868
  511.5 19.2 %copy-start.20 = (bf16[512,512]{1,0:T(8,128)(2,1)S(1)}, bf16[512,512]{1,0:T(8,128)(2,1)}, u32[]{:S(2)}) copy-start(bf16[512,512]{1,0:T(8,128)(2,1)} %copy-done.19) | copy-start | bytes 1572868
  511.5 20.6 %copy-start.30 = (bf16[512,512]{1,0:T(8,128)(2,1)S(1)}, bf16[512,512]{1,0:T(8,128)(2,1)}, u32[]{:S(2)}) copy-start(bf16[512,512]{1,0:T(8,128)(2,1)} %get-tuple-element.210) | copy-start | bytes 1572868
  511.6 20.6 %copy-start.37 = (f32[512]{0:T(512)S(1)}, f32[512]{0:T(512)}, u32[]{:S(2)}) copy-start(f32[512]{0:T(512)} %copy-done.36) | copy-start | bytes 6148
  511.6 20.6 %copy-start.39 = (f32[512]{0:T(512)S(1)}, f32[512]{0:T(512)}, u32[]{:S(2)}) copy-start(f32[512]{0:T(512)} %copy-done.38) | copy-start | bytes 6148
  511.6 20.6 %copy-start.41 = (f32[512]{0:T(512)S(1)}, f32[512]{0:T(512)}, u32[]{:S(2)}) copy-start(f32[512]{0:T(512)} %param.28) | copy-start | bytes 6148
  511.6 20.6 %copy-start.49 = (f32[512]{0:T(512)S(1)}, f32[512]{0:T(512)}, u32[]{:S(2)}) copy-start(f32[512]{0:T(512)} %param.29) | copy-start | bytes 6148
  511.6 115.4 %reduce-scatter.11.cloned.1.call-start = ((), (), s32[]{:S(2)}) async-start(), calls=%async_computation.11 | async-start | bytes 2621440 | tf_op jit(solution)/shard_map/reduce_scatter | solution.py:210
  515.8 251.5 %all-reduce.6.cloned.1.call-start = ((), (), s32[]{:S(2)}) async-start(), calls=%async_computation.12 | async-start | bytes 4194304 | tf_op jit(solution)/shard_map/psum | solution.py:243
  532.2 94.8 %copy-start.31 = (bf16[512,512]{1,0:T(8,128)(2,1)S(1)}, bf16[512,512]{1,0:T(8,128)(2,1)}, u32[]{:S(2)}) copy-start(bf16[512,512]{1,0:T(8,128)(2,1)} %get-tuple-element.210) | copy-start | bytes 1572868
  532.2 96.7 %copy-start.43 = (f32[512]{0:T(512)S(1)}, f32[512]{0:T(512)}, u32[]{:S(2)}) copy-start(f32[512]{0:T(512)} %copy-done.42) | copy-start | bytes 6148
  533.9 95.6 %copy-start.6 = (f32[512,512]{1,0:T(8,128)S(1)}, f32[512,512]{1,0:T(8,128)}, u32[]{:S(2)}) copy-start(f32[512,512]{1,0:T(8,128)} %get-tuple-element.244) | copy-start | bytes 3145732
  533.9 95.6 %copy-start.8 = (f32[512,512]{1,0:T(8,128)S(1)}, f32[512,512]{1,0:T(8,128)}, u32[]{:S(2)}) copy-start(f32[512,512]{1,0:T(8,128)} %copy-done.7) | copy-start | bytes 3145732
  582.7 184.6 %copy-start.33 = (f32[128,512]{1,0:T(8,128)S(1)}, f32[128,512]{1,0:T(8,128)}, u32[]{:S(2)}) copy-start(f32[128,512]{1,0:T(8,128)} %get-tuple-element.440) | copy-start | bytes 786436
  631.0 141.5 %copy-start.23 = (f32[512,512]{1,0:T(8,128)S(1)}, f32[512,512]{1,0:T(8,128)}, u32[]{:S(2)}) copy-start(f32[512,512]{1,0:T(8,128)} %get-tuple-element.448) | copy-start | bytes 3145732
  767.3 6.2 copy-start.24
  767.3 7.2 copy-start.1
  (18 other events, 39.9 us)
Sparse Core Ops, SparseCore 0:
  12.1 48.5 all-gather.4
  100.1 75.6 reduce-scatter.4
  180.9 46.4 all-gather.6
  229.5 44.6 all-gather.8
  285.3 42.5 reduce-scatter.6
  330.0 43.1 reduce-scatter.8
  379.4 45.2 all-gather.10
  511.6 69.0 all-reduce.7
  583.0 43.9 reduce-scatter.10
  633.9 133.3 all-reduce.5
where the time goes:
time: 792 us; the launch traced here: 782 us
  waiting for transfers between devices  509 us (64%)
  matrix products  89.2 us (11%)
  local copies, waits for them, and re-layouts  75.4 us (10%)
  blocking collectives  54.8 us (7%)
  other arithmetic  36.6 us (5%)
  between operations  15.2 us (2%)
    psum x1, waiting for transfers between devices, shards(): lax.psum((grad_gate_one_weight, grad_gate_one_bias, grad_output_bias, gra...  96.4 us
    reduce_scatter x1, waiting for transfers between devices, shards(): lax.psum_scatter(jnp.dot(context, output_weight, preferred_element_type=j...  75.7 us
    psum x1, waiting for transfers between devices, shards(): lax.psum((grad_joined_weight, grad_output_weight, grad_up_weight, grad_up...  46.8 us
    reduce_scatter x1, waiting for transfers between devices, shards(): lax.psum_scatter(contract_cols(grad_joined, joined_weight).astype(jnp.bfl...  44.3 us
    all_gather x1, waiting for transfers between devices, shards(): rows_two = lax.all_gather(rounded_two, 'mp', axis=0, tiled=True)  43.5 us
    reduce_scatter x1, waiting for transfers between devices, shards(): lax.psum_scatter(contract_cols(pre_low, up_weight).astype(jnp.bfloat16),...  42.7 us
    dynamic_update_slice x8, local copies, waits for them, and re-layouts, shards(): lax.map(attend_backward, (query, keys, values, doc_ids, logsum, grad_cont...  42.1 us
    all_gather x1, waiting for transfers between devices, shards(): lax.all_gather(grad_branch.astype(jnp.bfloat16), 'mp', axis=0, tiled=True)  42 us
  transfers between devices with their start and end apart: 10, of which 10 were waited for; matrix products, arithmetic and copies ran while one was open for 5% of the time, Pallas kernels for 0%

commit v1 on v0

v1 whole, which is shorter than its diff:
```python
import functools
import math
from types import SimpleNamespace

import jax
import jax.numpy as jnp
import numpy as np
from jax import lax
from jax.experimental import pallas as pl
from jax.experimental.pallas import tpu as pltpu
from jax.sharding import PartitionSpec as P

BF = jnp.bfloat16
F32 = jnp.float32
MESH = pl.DeviceIdType.MESH
D = 512
T = 512
S = 1024
HD = 64
CH = 256
NCOPY = 128
GELU_A = math.sqrt(2.0 / math.pi)
GELU_B = 0.044715


def mm(a, b):
    return lax.dot_general(a, b, (((1,), (0,)), ((), ())), preferred_element_type=F32)


def mmt(a, b):
    return lax.dot_general(a, b, (((1,), (1,)), ((), ())), preferred_element_type=F32)


def tmm(a, b):
    return lax.dot_general(a, b, (((0,), (0,)), ((), ())), preferred_element_type=F32)


def sigmoid(v):
    return 0.5 * jnp.tanh(0.5 * v) + 0.5


def colsum(v):
    return jnp.sum(v, axis=0, keepdims=True)


def rowmean(v):
    return jnp.mean(v, axis=-1, keepdims=True)


OUT_SHAPES = dict(
    o_out=((T, D), BF),
    o_gt=((T, D), F32),
    o_a=((8, 64, 512), BF),
    o_u=((8, 128, 256), BF),
    o_d=((8, 64, 512), BF),
    o_g1=((8, 4, 32, 256), BF),
    o_g2=((8, 4, 32, 256), BF),
    o_vec=((16, 512), F32),
)

SCRATCH = dict(
    xt=((T, D), BF), ct=((T, D), BF),
    info=((2, 8, S), F32), dcol=((S, 128), F32), drow=((8, S), F32),
    ctb=((S, 128), F32), stb=((S, 128), F32), cttb=((128, S), F32), sttb=((128, S), F32),
    wz=((4, 256, 512), BF), wt=((768, 512), BF), wo=((256, 512), BF),
    upz=((4, 512, 256), BF), dnz=((4, 256, 512), BF), ubz=((4, 8, 256), F32),
    n1=((S, D), BF), xh1=((T, D), F32), rs1=((T, 128), F32), g1=((T, D), F32),
    q=((S, 256), BF), k=((S, 256), BF), v=((S, 256), BF),
    km=((4, S, 256), BF), vm=((4, S, 256), BF),
    bias=((CH, 768), F32), pr=((4, CH, 2304), BF), ctx=((S, 256), BF),
    xs=((T, D), F32), xr=((T, D), F32), amx=((T, D), F32), mid=((T, D), F32),
    xh2=((T, D), F32), rs2=((T, 128), F32), n2=((S, D), BF),
    hid=((S, 1024), BF), gp=((S, 1024), BF),
    outb=((T, D), BF),
    bl=((S, D), BF), go2=((T, D), BF), gl2=((S, 256), BF),
    al=((S, D), BF), go1=((T, D), BF), gl1=((S, 256), BF),
    gmr=((T, D), F32),
    dc=((S, 256), BF), dct=((256, S), BF), qt=((256, S), BF),
    dkt=((256, S), F32), dvt=((256, S), F32), dq=((S, 768), BF), dt=((768, S), BF),
    a_s=((4, 256, 512), BF), a_a=((3, 4, 64, 512), BF), a_b=((4, 64, 512), BF), a_c=((3, 64, 512), BF),
    u_s=((4, 512, 256), BF), u_a=((3, 4, 128, 256), BF), u_b=((4, 128, 256), BF), u_c=((3, 128, 256), BF),
    d_s=((4, 256, 512), BF), d_a=((3, 4, 64, 512), BF), d_b=((4, 64, 512), BF), d_c=((3, 64, 512), BF),
    e_s=((4, 128, 256), BF), e_a=((3, 4, 32, 256), BF), e_b=((4, 32, 256), BF), e_c=((3, 32, 256), BF),
    f_s=((4, 128, 256), BF), f_a=((3, 4, 32, 256), BF), f_b=((4, 32, 256), BF), f_c=((3, 32, 256), BF),
    pk=((16, 512), F32), pk1=((2, 16, 512), F32), pk2=((4, 16, 512), F32), pk3=((4, 16, 512), F32),
)


def kernel(ndp, xbits, names, *refs):
    R = SimpleNamespace(**dict(zip(names, refs)))
    dp = lax.axis_index("dp")
    m = lax.axis_index("mp")
    bits = [lax.rem(lax.div(dp, 1 << b), 2) for b in range(ndp.bit_length() - 1)]
    c = bits[0]
    g = bits[1] + 2 * bits[2]
    mb = [lax.rem(m, 2), lax.div(m, 2)]

    def dpx(mask):
        value = dp
        for b in range(len(bits)):
            if mask >> b & 1:
                value = value + (1 - 2 * bits[b]) * (1 << b)
        return value

    def mx(mask):
        value = m
        for b in range(2):
            if mask >> b & 1:
                value = value + (1 - 2 * mb[b]) * (1 << b)
        return value

    def gx(mask):
        value = g
        for b in range(2):
            if mask >> b & 1:
                value = value + (1 - 2 * bits[1 + b]) * (1 << b)
        return value

    swap = (c + mb[0]) == 1
    r0 = pl.multiple_of(c * T, T)
    p0 = pl.multiple_of(T - c * T, T)
    slot = c + 2 * g
    counter = [0]

    def remote(src, dst, device):
        index = counter[0]
        counter[0] += 1
        return pltpu.make_async_remote_copy(
            src_ref=src, dst_ref=dst, send_sem=R.ss.at[index], recv_sem=R.rs.at[index],
            device_id=device, device_id_type=MESH,
        )

    def local(src, dst, index):
        return pltpu.make_async_copy(src, dst, R.ls.at[index])

    partner = (dpx(1), m)
    cross = (dpx(1), mx(1))
    barrier = pltpu.get_barrier_semaphore()
    friends = [(dpx(k), m) for k in range(1, 8)] + [(dp, mx(k)) for k in (1, 2, 3)] + [cross]
    friends += [(dpx(1 << b), m) for b in range(3, 3 + xbits)]
    for friend in friends:
        pl.semaphore_signal(barrier, inc=1, device_id=friend, device_id_type=MESH)
    own_up = local(R.up.at[:, pl.ds(pl.multiple_of(c * 256, 256), 256)], R.upz.at[m], 0)
    own_dn = local(R.down.at[pl.ds(pl.multiple_of(c * 256, 256), 256), :], R.dnz.at[m], 1)
    own_up.start()
    own_dn.start()
    loc_x = local(R.tokens, R.xt, 2)
    loc_c = local(R.cot, R.ct, 3)

    @pl.when(jnp.logical_not(swap))
    def _():
        loc_x.start()
        loc_c.start()

    lane = lax.broadcasted_iota(jnp.int32, (64, 128), 1)
    pick = (lane == lax.broadcasted_iota(jnp.int32, (64, 128), 0) + c * 64)
    pick = jnp.where(pick, 1.0, 0.0).astype(BF)
    wz = R.wz
    wz[m, 0:64, :] = mmt(pick, R.qw[...]).astype(BF)
    wz[m, 64:128, :] = mmt(pick, R.kw[...]).astype(BF)
    wz[m, 128:192, :] = mmt(pick, R.vw[...]).astype(BF)
    wz[m, 192:256, :] = R.ow[pl.ds(pl.multiple_of(c * 64, 64), 64), :]
    ubv = R.ub[...]
    ubv = jnp.where(c == 0, ubv[:, :256], ubv[:, 256:])
    R.ubz[m] = jnp.broadcast_to(ubv, (8, 256))
    info = R.info
    fl = lax.broadcasted_iota(jnp.int32, (2, 128), 1)
    freq = jnp.exp(lax.rem(fl, 32).astype(F32) * (-2.0 * math.log(10000.0) / HD))
    turn = jnp.where(
        lax.broadcasted_iota(jnp.int32, (2, 128), 0) == 0, R.resets[0:1, 0:1], R.resets[0:1, 1:2]
    ).astype(F32)
    info[0] = jnp.zeros((8, S), F32)
    info[0, 0:2, :] = R.docs[...].astype(F32)
    info[0, 2:4, 0:128] = jnp.cos(turn * freq)
    info[0, 2:4, 128:256] = jnp.sin(turn * freq)
    info[0, 2:4, 256:384] = turn

    pl.semaphore_wait(barrier, len(friends))

    swap_x = remote(R.tokens, R.xt, cross)
    swap_c = remote(R.cot, R.ct, cross)

    @pl.when(swap)
    def _():
        swap_x.start()

    w_1 = remote(wz.at[m], wz.at[m], (dp, mx(1)))
    w_3 = remote(wz.at[m], wz.at[m], (dp, mx(3)))
    w_3.start()
    w_1.start()
    send_info = remote(info.at[0], info.at[1], partner)
    send_info.start()
    ub_copies = [remote(R.ubz.at[m], R.ubz.at[m], (dp, mx(k))) for k in (1, 2, 3)]
    for copy in ub_copies:
        copy.start()

    send_info.wait()
    row = mb[1]
    mine = jnp.where(swap, 0.0, 1.0)

    def info_row(i):
        return info[0, pl.ds(i, 1), :] * mine + info[1, pl.ds(i, 1), :] * (1.0 - mine)

    doc = info_row(row)
    turn_row = info_row(row + 2)
    R.drow[...] = jnp.broadcast_to(doc, (8, S))
    R.dcol[...] = jnp.broadcast_to(doc, (128, S)).T
    cr, sr, rr = turn_row[:, 0:128], turn_row[:, 128:256], turn_row[:, 256:384]

    @pl.loop(0, 4)
    def _(i):
        rows = pl.ds(pl.multiple_of(i * CH, CH), CH)
        c0, s0 = R.ctab[rows, :], R.stab[rows, :]
        place = (lax.broadcasted_iota(jnp.int32, (CH, 128), 0) + i * CH).astype(F32)
        past = place >= rr
        cc = jnp.where(past, c0 * cr + s0 * sr, c0)
        sn = jnp.where(past, s0 * cr - c0 * sr, s0)
        R.ctb[rows, :] = cc
        R.stb[rows, :] = sn
        R.cttb[:, rows] = cc.T
        R.sttb[:, rows] = sn.T

    @pl.when(jnp.logical_not(swap))
    def _():
        loc_x.wait()
        loc_c.wait()

    @pl.when(swap)
    def _():
        swap_x.wait()

    n1 = R.n1

    @pl.loop(0, 2)
    def _(i):
        rows = pl.ds(pl.multiple_of(i * CH, CH), CH)
        x = R.xt[rows, :].astype(F32)
        x = x - rowmean(x)
        rstd = lax.rsqrt(rowmean(x * x) + 1e-05)
        xh = x * rstd
        R.xh1[rows, :] = xh
        R.rs1[rows, :] = jnp.broadcast_to(rstd, (CH, 128))
        n1[pl.ds(pl.multiple_of(r0 + i * CH, CH), CH), :] = (xh * R.n1g[...] + R.n1b[...]).astype(BF)

    own_rows = pl.ds(r0, T)
    partner_rows = pl.ds(p0, T)
    send_n1 = remote(n1.at[own_rows, :], n1.at[own_rows, :], partner)
    send_n1.start()

    @pl.loop(0, 2)
    def _(i):
        rows = pl.ds(pl.multiple_of(i * CH, CH), CH)
        gate = mm(n1[pl.ds(pl.multiple_of(r0 + i * CH, CH), CH), :], R.wg1[...]) + R.g1b[...]
        R.g1[rows, :] = sigmoid(gate)

    w_1.wait_recv()
    w_3.wait_recv()
    relay_3 = remote(wz.at[mx(1), 0:128, :], wz.at[mx(1), 0:128, :], (dp, mx(3)))
    relay_1 = remote(wz.at[mx(3), 128:256, :], wz.at[mx(3), 128:256, :], (dp, mx(1)))
    relay_3.start()
    relay_1.start()
    own_up.wait()
    own_dn.wait()
    upz, dnz = R.upz, R.dnz
    relay_3.wait_recv()
    relay_1.wait_recv()
    ff = []
    for z in (upz, dnz):
        for k in (3, 1):
            ff.append(remote(z.at[m], z.at[m], (dp, mx(k))))
    for copy in ff:
        copy.start()

    @pl.when(swap)
    def _():
        swap_c.start()

    wt = R.wt
    for z in range(4):
        wt[z * 32 : z * 32 + 32, :] = wz[z, 0:32, :]
        wt[128 + z * 32 : 160 + z * 32, :] = wz[z, 32:64, :]
        wt[256 + z * 32 : 288 + z * 32, :] = wz[z, 64:96, :]
        wt[384 + z * 32 : 416 + z * 32, :] = wz[z, 96:128, :]
        wt[512 + z * 64 : 576 + z * 64, :] = wz[z, 128:192, :]
        R.wo[z * 64 : z * 64 + 64, :] = wz[z, 192:256, :]

    flane = lax.broadcasted_iota(jnp.int32, (1, 256), 1)
    qmask = [jnp.where(lax.div(lax.rem(flane, 128), 32) == h, 1.0, 0.0).astype(BF) for h in range(4)]
    vmask = [jnp.where(lax.div(flane, 64) == h, 1.0, 0.0).astype(BF) for h in range(4)]

    def project(base):
        @pl.loop(0, 2)
        def _(i):
            rows = pl.ds(pl.multiple_of(base + i * CH, CH), CH)
            both = mmt(n1[rows, :], wt[...])
            cc, sn = R.ctb[rows, :], R.stb[rows, :]
            qa, qb = both[:, 0:128], both[:, 128:256]
            ka, kb = both[:, 256:384], both[:, 384:512]
            qq = jnp.concatenate([qa * cc - qb * sn, qb * cc + qa * sn], axis=1).astype(BF)
            kk = jnp.concatenate([ka * cc - kb * sn, kb * cc + ka * sn], axis=1).astype(BF)
            vv = both[:, 512:768].astype(BF)
            R.q[rows, :] = qq * jnp.asarray(0.125, BF)
            R.k[rows, :] = kk
            R.v[rows, :] = vv
            for h in range(4):
                R.km[h, rows, :] = kk * qmask[h]
                R.vm[h, rows, :] = vv * vmask[h]

    project(r0)
    send_n1.wait()
    project(p0)

    relays = []
    for j, (z, half) in enumerate(((upz, 256), (dnz, 128))):
        ff[2 * j].wait_recv()
        ff[2 * j + 1].wait_recv()
        relays.append(remote(z.at[mx(1), 0:half, :], z.at[mx(1), 0:half, :], (dp, mx(3))))
        relays.append(remote(z.at[mx(3), half : 2 * half, :], z.at[mx(3), half : 2 * half, :], (dp, mx(1))))
    for copy in relays:
        copy.start()

    def span(i):
        width = min(i + 1, 3) * CH
        return (i + 1) * CH - width, width

    def lead(i):
        return sum(span(j)[1] for j in range(i))

    for i in range(4):
        j0, width = span(i)
        rows = slice(i * CH, (i + 1) * CH)
        dcol = R.dcol[rows, :]
        qi = lax.broadcasted_iota(jnp.int32, (CH, 128), 0) + i * CH
        for w in range(width // 128):
            ki = lax.broadcasted_iota(jnp.int32, (CH, 128), 1) + (j0 + w * 128)
            ok = (dcol == R.drow[0:1, j0 + w * 128 : j0 + w * 128 + 128]) & (ki <= qi)
            R.bias[:, w * 128 : w * 128 + 128] = jnp.where(ok, 0.0, -1e30)
        qr = R.q[rows, :]
        total = jnp.zeros((CH, 256), F32)
        for h in range(4):
            sc = mmt(qr * qmask[h], R.k[j0 : j0 + width, :]) + R.bias[:, 0:width]
            e = jnp.exp(sc - jnp.max(sc, axis=-1, keepdims=True))
            p = (e * (1.0 / jnp.sum(e, axis=-1, keepdims=True))).astype(BF)
            R.pr[h, :, lead(i) : lead(i) + width] = p
            total = total + mm(p, R.vm[h, j0 : j0 + width, :])
        R.ctx[rows, :] = total.astype(BF)

    def chunks(body):
        pl.loop(0, 2)(body)

    def at(base, i):
        return pl.ds(pl.multiple_of(base + i * CH, CH), CH)

    @chunks
    def _(i):
        R.xs[at(0, i), :] = mm(R.ctx[at(p0, i), :], R.wo[...])

    send_at = remote(R.xs, R.xr, partner)
    send_at.start()

    @chunks
    def _(i):
        R.amx[at(0, i), :] = mm(R.ctx[at(r0, i), :], R.wo[...])

    send_at.wait()
    n2 = R.n2

    @chunks
    def _(i):
        rows = at(0, i)
        x = R.xt[rows, :].astype(F32)
        amx = R.amx[rows, :] + R.xr[rows, :] + R.ob[...] - x
        R.amx[rows, :] = amx
        mid = x + R.g1[rows, :] * amx
        R.mid[rows, :] = mid
        mid = mid - rowmean(mid)
        rstd = lax.rsqrt(rowmean(mid * mid) + 1e-05)
        xh = mid * rstd
        R.xh2[rows, :] = xh
        R.rs2[rows, :] = jnp.broadcast_to(rstd, (CH, 128))
        n2[at(r0, i), :] = (xh * R.n2g[...] + R.n2b[...]).astype(BF)

    send_n2 = remote(n2.at[own_rows, :], n2.at[own_rows, :], partner)
    send_n2.start()
    for copy in relays + ub_copies:
        copy.wait_recv()

    def up_part(base):
        @chunks
        def _(i):
            rows = at(base, i)
            a = n2[rows, :]
            for z in range(4):
                v = mm(a, upz[z]) + R.ubz[z, 0:1, :]
                v2 = v * v
                t = jnp.tanh(GELU_A * v * (1.0 + GELU_B * v2))
                half = 0.5 * (1.0 + t)
                R.hid[rows, z * 256 : z * 256 + 256] = (v * half).astype(BF)
                slope = half + (0.5 * GELU_A) * v * (1.0 - t * t) * (1.0 + (3.0 * GELU_B) * v2)
                R.gp[rows, z * 256 : z * 256 + 256] = slope.astype(BF)

    def down_part(base, dst):
        @chunks
        def _(i):
            rows = at(base, i)
            total = mm(R.hid[rows, 0:256], dnz[0])
            for z in range(1, 4):
                total = total + mm(R.hid[rows, z * 256 : z * 256 + 256], dnz[z])
            dst[at(0, i), :] = total

    up_part(r0)
    send_n2.wait()
    up_part(p0)
    down_part(p0, R.xs)
    send_br = remote(R.xs, R.xr, partner)
    send_br.start()
    down_part(r0, R.gmr)

    @pl.when(swap)
    def _():
        swap_c.wait()

    pk = R.pk
    pk[...] = jnp.zeros((16, 512), F32)
    send_br.wait()

    @chunks
    def _(i):
        rows = at(0, i)
        gate = sigmoid(mm(n2[at(r0, i), :], R.wg2[...]) + R.g2b[...])
        mid = R.mid[rows, :]
        bm = R.gmr[rows, :] + R.xr[rows, :] + R.db[...] - mid
        R.outb[rows, :] = (mid + gate * bm).astype(BF)
        cot = R.ct[rows, :].astype(F32)
        gb = gate * cot
        rest = cot - gb
        R.mid[rows, :] = rest
        gg = rest * bm * gate
        R.bl[at(r0, i), :] = gb.astype(BF)
        R.go2[rows, :] = gg.astype(BF)
        pk[6:7, :] += colsum(gb)
        pk[7:8, :] += colsum(gg)

    mine_cols = pl.ds(pl.multiple_of(c * 256, 256), 256)
    their_cols = pl.ds(pl.multiple_of(256 - c * 256, 256), 256)
    send_bl = remote(R.bl.at[own_rows, :], R.bl.at[own_rows, :], partner)
    send_bl.start()
    send_gl2 = remote(R.go2.at[:, their_cols], R.gl2.at[own_rows, :], partner)
    send_gl2.start()
    keep_gl2 = local(R.go2.at[:, mine_cols], R.gl2.at[own_rows, :], 4)
    keep_gl2.start()
    back_o = remote(R.outb, R.o_out, cross)
    keep_o = local(R.outb, R.o_out, 5)

    @pl.when(swap)
    def _():
        back_o.start()

    @pl.when(jnp.logical_not(swap))
    def _():
        keep_o.start()

    def hidden_back(base):
        sums = []
        for z in range(4):
            lanes = slice(z * 256, z * 256 + 256)

            def step(i, acc, lanes=lanes, z=z):
                rows = at(base, i)
                gpre = mmt(R.bl[rows, :], dnz[z]) * R.gp[rows, lanes].astype(F32)
                R.gp[rows, lanes] = gpre.astype(BF)
                return acc + colsum(gpre)

            both = lax.fori_loop(0, 2, step, jnp.zeros((1, 256), F32))
            pk[8 + z : 9 + z, 0:256] += jnp.where(c == 0, both, 0.0)
            pk[8 + z : 9 + z, 256:512] += jnp.where(c == 0, 0.0, both)

    def norm_two_part(base, dst):
        @chunks
        def _(i):
            rows = at(base, i)
            total = mmt(R.gp[rows, 0:256], upz[0])
            for z in range(1, 4):
                total = total + mmt(R.gp[rows, z * 256 : z * 256 + 256], upz[z])
            dst[at(0, i), :] = total

    hidden_back(r0)
    send_bl.wait()
    hidden_back(p0)
    norm_two_part(p0, R.xs)
    send_d2 = remote(R.xs, R.xr, partner)
    send_d2.start()
    norm_two_part(r0, R.gmr)

    def reduce_start(name, quarter):
        out = []
        for k in (1, 2, 3):
            rows = pl.ds(pl.multiple_of(gx(k) * quarter, quarter), quarter)
            copy = remote(getattr(R, name + "_s").at[:, rows, :], getattr(R, name + "_a").at[k - 1], (dpx(2 * k), m))
            copy.start()
            out.append(copy)
        return out

    def reduce_middle(name, quarter, copies):
        for copy in copies:
            copy.wait()
        rows = pl.ds(pl.multiple_of(g * quarter, quarter), quarter)
        for z in range(4):
            total = getattr(R, name + "_s")[z, rows, :].astype(F32)
            for k in range(3):
                total = total + getattr(R, name + "_a")[k, z].astype(F32)
            getattr(R, name + "_b")[z] = total.astype(BF)
        out = []
        for k in (1, 2, 3):
            copy = remote(getattr(R, name + "_b").at[mx(k)], getattr(R, name + "_c").at[k - 1], (dp, mx(k)))
            copy.start()
            out.append(copy)
        return out

    def reduce_total(name, copies):
        for copy in copies:
            copy.wait()
        total = getattr(R, name + "_b")[m].astype(F32)
        for k in range(3):
            total = total + getattr(R, name + "_c")[k].astype(F32)
        for b in range(xbits):
            getattr(R, name + "_x")[2 * b] = total.astype(BF)
            copy = remote(getattr(R, name + "_x").at[2 * b], getattr(R, name + "_x").at[2 * b + 1], (dpx(8 << b), m))
            copy.start()
            copy.wait()
            total = getattr(R, name + "_x")[2 * b].astype(F32) + getattr(R, name + "_x")[2 * b + 1].astype(F32)
        return total.astype(BF)

    def spread(out):
        copies = []
        for k in range(1, 8):
            copy = remote(out.at[slot], out.at[slot], (dpx(k), m))
            copy.start()
            copies.append(copy)
        return copies

    def reduce_end(name, out, copies):
        out[slot] = reduce_total(name, copies)
        return spread(out)

    def reduce_end_all(name, out, copies):
        out[slot, m] = reduce_total(name, copies)
        copies = []
        for k in (1, 2, 3):
            copy = remote(out.at[slot, m], out.at[slot, m], (dp, mx(k)))
            copy.start()
            copies.append(copy)
        return copies

    for z in range(4):
        R.d_s[z] = tmm(R.hid[:, z * 256 : z * 256 + 256], R.bl[...]).astype(BF)
    d_1 = reduce_start("d", 64)
    n2t = n2[...].T
    for z in range(4):
        R.u_s[z] = mm(n2t, R.gp[:, z * 256 : z * 256 + 256]).astype(BF)
    u_1 = reduce_start("u", 128)
    send_gl2.wait()
    keep_gl2.wait()
    full = mm(n2t, R.gl2[...]).astype(BF)
    for z in range(4):
        R.e_s[z] = full[z * 128 : z * 128 + 128, :]
    e_1 = reduce_start("e", 32)

    send_d2.wait()

    @chunks
    def _(i):
        rows = at(0, i)
        gn = R.gmr[rows, :] + R.xr[rows, :] + mmt(R.go2[rows, :], R.wg2[...])
        xh = R.xh2[rows, :]
        pk[4:5, :] += colsum(gn * xh)
        pk[5:6, :] += colsum(gn)
        e = gn * R.n2g[...]
        gm = R.rs2[rows, 0:1] * (e - rowmean(e) - xh * rowmean(e * xh)) + R.mid[rows, :]
        gate = R.g1[rows, :]
        ga = gate * gm
        gg = (gm - ga) * R.amx[rows, :] * gate
        R.mid[rows, :] = gm - ga
        R.al[at(r0, i), :] = ga.astype(BF)
        R.go1[rows, :] = gg.astype(BF)
        pk[2:3, :] += colsum(ga)
        pk[3:4, :] += colsum(gg)

    send_al = remote(R.al.at[own_rows, :], R.al.at[own_rows, :], partner)
    send_al.start()
    send_gl1 = remote(R.go1.at[:, their_cols], R.gl1.at[own_rows, :], partner)
    send_gl1.start()
    keep_gl1 = local(R.go1.at[:, mine_cols], R.gl1.at[own_rows, :], 6)
    keep_gl1.start()
    R.qt[...] = R.q[...].T
    n1t = n1[...].T
    send_al.wait()

    @pl.loop(0, 4)
    def _(i):
        rows = at(0, i)
        a = R.al[rows, :]
        R.dc[rows, :] = mmt(a, R.wo[...]).astype(BF)
        R.dct[:, rows] = mmt(R.wo[...], a).astype(BF)

    grad_wo = tmm(R.ctx[...], R.al[...]).astype(BF)
    for z in range(4):
        R.a_s[z, 192:256, :] = grad_wo[z * 64 : z * 64 + 64, :]
    send_gl1.wait()
    keep_gl1.wait()
    full = mm(n1t, R.gl1[...]).astype(BF)
    for z in range(4):
        R.f_s[z] = full[z * 128 : z * 128 + 128, :]
    f_1 = reduce_start("f", 32)

    dkt, dvt = R.dkt, R.dvt
    dkt[...] = jnp.zeros((256, S), F32)
    dvt[...] = jnp.zeros((256, S), F32)
    for i in range(4):
        j0, width = span(i)
        rows = slice(i * CH, (i + 1) * CH)
        keys = slice(j0, j0 + width)
        dcr = R.dc[rows, :]
        total = jnp.zeros((CH, 256), F32)
        for h in range(4):
            p = R.pr[h, :, lead(i) : lead(i) + width]
            pf = p.astype(F32)
            t = mmt(dcr * vmask[h], R.v[keys, :]) * pf
            ds = (t - pf * jnp.sum(t, axis=-1, keepdims=True)).astype(BF)
            total = total + mm(ds, R.km[h, keys, :])
            dvt[h * 64 : h * 64 + 64, keys] += mm(R.dct[h * 64 : h * 64 + 64, rows], p)
            qh = jnp.concatenate(
                [R.qt[h * 32 : h * 32 + 32, rows], R.qt[128 + h * 32 : 160 + h * 32, rows]], axis=0
            )
            dk = mm(qh, ds)
            dkt[h * 32 : h * 32 + 32, keys] += dk[0:32]
            dkt[128 + h * 32 : 160 + h * 32, keys] += dk[32:64]
        total = total * 0.125
        a, b = total[:, 0:128], total[:, 128:256]
        cc, sn = R.ctb[rows, :], R.stb[rows, :]
        R.dq[rows, 0:256] = jnp.concatenate([a * cc + b * sn, b * cc - a * sn], axis=1).astype(BF)
        if i == 1:
            d_2 = reduce_middle("d", 64, d_1)
            u_2 = reduce_middle("u", 128, u_1)
            e_2 = reduce_middle("e", 32, e_1)
        if i == 2:
            d_3 = reduce_end("d", R.o_d, d_2)
            u_3 = reduce_end("u", R.o_u, u_2)
            e_3 = reduce_end_all("e", R.o_g2, e_2)
    f_2 = reduce_middle("f", 32, f_1)

    dt = R.dt
    dt[512:768, :] = dvt[...].astype(BF)
    a, b = dkt[0:128, :], dkt[128:256, :]
    dt[256:384, :] = (a * R.cttb[...] + b * R.sttb[...]).astype(BF)
    dt[384:512, :] = (b * R.cttb[...] - a * R.sttb[...]).astype(BF)
    dt[0:256, :] = R.dq[:, 0:256].T
    R.dq[:, 256:768] = dt[256:768, :].T

    @chunks
    def _(i):
        R.xs[at(0, i), :] = mm(R.dq[at(p0, i), :], wt[...])

    send_d1 = remote(R.xs, R.xr, partner)
    send_d1.start()
    for part in range(3):
        grad = mm(dt[part * 256 : part * 256 + 256, :], n1[...]).astype(BF)
        for z in range(4):
            if part < 2:
                R.a_s[z, part * 64 : part * 64 + 32, :] = grad[z * 32 : z * 32 + 32, :]
                R.a_s[z, part * 64 + 32 : part * 64 + 64, :] = grad[128 + z * 32 : 160 + z * 32, :]
            else:
                R.a_s[z, 128:192, :] = grad[z * 64 : z * 64 + 64, :]
    a_1 = reduce_start("a", 64)

    for copy in e_3:
        copy.wait()
    e_4 = spread(R.o_g2)
    f_3 = reduce_end_all("f", R.o_g1, f_2)

    @chunks
    def _(i):
        R.gmr[at(0, i), :] = mm(R.dq[at(r0, i), :], wt[...])

    send_d1.wait()

    @chunks
    def _(i):
        rows = at(0, i)
        gn = R.gmr[rows, :] + R.xr[rows, :] + mmt(R.go1[rows, :], R.wg1[...])
        xh = R.xh1[rows, :]
        pk[0:1, :] += colsum(gn * xh)
        pk[1:2, :] += colsum(gn)
        e = gn * R.n1g[...]
        R.gmr[rows, :] = R.rs1[rows, 0:1] * (e - rowmean(e) - xh * rowmean(e * xh)) + R.mid[rows, :]

    back_t = remote(R.gmr, R.o_gt, cross)
    keep_t = local(R.gmr, R.o_gt, 7)

    pk1, pk2, pk3 = R.pk1, R.pk2, R.pk3
    pk1[c] = pk[...]
    p_1 = remote(pk1.at[c], pk1.at[c], partner)
    p_1.start()

    @pl.when(swap)
    def _():
        back_t.start()

    @pl.when(jnp.logical_not(swap))
    def _():
        keep_t.start()

    a_2 = reduce_middle("a", 64, a_1)
    p_1.wait()
    pk2[g] = pk1[0] + pk1[1]
    p_2 = [remote(pk2.at[g], pk2.at[g], (dpx(2 * k), m)) for k in (1, 2, 3)]
    for copy in p_2:
        copy.start()
    for copy in f_3:
        copy.wait()
    f_4 = spread(R.o_g1)
    for copy in p_2:
        copy.wait()
    pk3[m] = (pk2[0] + pk2[1]) + (pk2[2] + pk2[3])
    p_3 = [remote(pk3.at[m], pk3.at[m], (dp, mx(k))) for k in (1, 2, 3)]
    for copy in p_3:
        copy.start()
    a_3 = reduce_end("a", R.o_a, a_2)
    for copy in p_3:
        copy.wait()
    total = (pk3[0] + pk3[1]) + (pk3[2] + pk3[3])
    for b in range(xbits):
        R.p_x[2 * b] = total
        copy = remote(R.p_x.at[2 * b], R.p_x.at[2 * b + 1], (dpx(8 << b), m))
        copy.start()
        copy.wait()
        total = R.p_x[2 * b] + R.p_x[2 * b + 1]
    pk[...] = total
    R.o_vec[...] = total
    R.o_vec[8:9, :] = pk[pl.ds(8 + m, 1), :]

    for copy in [w_1, w_3, relay_1, relay_3] + ub_copies + ff + relays:
        copy.wait_send()
    for copy in d_3 + u_3 + e_4 + f_4 + a_3:
        copy.wait()

    @pl.when(swap)
    def _():
        back_o.wait()
        back_t.wait()

    @pl.when(jnp.logical_not(swap))
    def _():
        keep_o.wait()
        keep_t.wait()


def unpack(a, u, d, g1, g2, vec, out, gt, *outs):
    (oq, ok, ov, oo, ou, od, og1, og2, oout, ogt) = outs[:10]
    for j, ref in enumerate((oq, ok, ov)):
        both = jnp.concatenate([a[2 * j].astype(F32), a[2 * j + 1].astype(F32)], axis=0)
        ref[...] = both.T
    for c in range(2):
        oo[c * 64 : c * 64 + 64, :] = a[6 + c].astype(F32)
        for g in range(4):
            ou[g * 128 : g * 128 + 128, c * 256 : c * 256 + 256] = u[2 * g + c].astype(F32)
            od[c * 256 + g * 64 : c * 256 + g * 64 + 64, :] = d[2 * g + c].astype(F32)
            for z in range(4):
                rows = slice(z * 128 + g * 32, z * 128 + g * 32 + 32)
                og1[rows, c * 256 : c * 256 + 256] = g1[2 * g + c, z].astype(F32)
                og2[rows, c * 256 : c * 256 + 256] = g2[2 * g + c, z].astype(F32)
    oout[...] = out[...]
    ogt[...] = gt[...]
    for j, ref in enumerate(outs[10:]):
        ref[...] = vec[j : j + 1, :]


def tables():
    freqs = np.exp(np.arange(HD // 2, dtype=np.float32) * np.float32(-2.0 * math.log(10000.0) / HD))
    angles = np.arange(S, dtype=np.float32)[:, None] * freqs.astype(np.float32)
    angles = np.tile(angles.astype(np.float64), (1, 4))
    return np.cos(angles).astype(np.float32), np.sin(angles).astype(np.float32)


def shards(
    ndp, tokens, doc_ids, resets, n1g, n1b, qw, kw, vw, ow, ob, wg1, g1b, n2g, n2b, up, ub, down, db,
    wg2, g2b, cot,
):
    xbits = ndp.bit_length() - 4
    ctab, stab = tables()
    vector = lambda v: v.reshape(1, -1)
    values = dict(
        tokens=tokens, cot=cot, docs=doc_ids, resets=resets.reshape(1, 2), qw=qw, kw=kw, vw=vw, ow=ow,
        wg1=wg1, up=up, down=down, wg2=wg2, n1g=vector(n1g), n1b=vector(n1b), ob=vector(ob),
        g1b=vector(g1b), n2g=vector(n2g), n2b=vector(n2b), ub=vector(ub), db=vector(db), g2b=vector(g2b),
        ctab=jnp.asarray(ctab), stab=jnp.asarray(stab),
    )
    vmem = pl.BlockSpec(memory_space=pltpu.VMEM)
    anyspace = pl.BlockSpec(memory_space=pl.ANY)
    scratch = {name: pltpu.VMEM(shape, dtype) for name, (shape, dtype) in SCRATCH.items()}
    if xbits:
        more = dict(a_x=(64, 512), u_x=(128, 256), d_x=(64, 512), e_x=(32, 256), f_x=(32, 256))
        for name, shape in more.items():
            scratch[name] = pltpu.VMEM((2 * xbits,) + shape, BF)
        scratch.update(p_x=pltpu.VMEM((2 * xbits, 16, 512), F32))
    copies = pltpu.SemaphoreType.DMA((NCOPY + 6 * xbits,))
    scratch.update(ss=copies, rs=copies, ls=pltpu.SemaphoreType.DMA((8,)))
    in_specs = dict.fromkeys(values, vmem)
    in_specs.update(tokens=anyspace, cot=anyspace, up=anyspace, down=anyspace)
    packed = pl.pallas_call(
        functools.partial(kernel, ndp, xbits, (*values, *OUT_SHAPES, *scratch)),
        out_shape=[jax.ShapeDtypeStruct(shape, dtype) for shape, dtype in OUT_SHAPES.values()],
        in_specs=list(in_specs.values()),
        out_specs=[vmem] * len(OUT_SHAPES),
        scratch_shapes=list(scratch.values()),
        compiler_params=pltpu.CompilerParams(
            collective_id=0, has_side_effects=True, vmem_limit_bytes=64 << 20
        ),
        name="block",
    )(*values.values())
    out, gt, a, u, d, g1, g2, vec = packed
    f32 = lambda *shape: jax.ShapeDtypeStruct(shape, F32)
    shapes = [f32(D, 128)] * 3 + [f32(128, D)] + [f32(D, D)] * 4
    shapes += [jax.ShapeDtypeStruct((T, D), BF), f32(T, D)] + [f32(1, D)] * 9
    res = pl.pallas_call(
        unpack,
        out_shape=shapes,
        in_specs=[vmem] * 8,
        out_specs=[vmem] * len(shapes),
        compiler_params=pltpu.CompilerParams(vmem_limit_bytes=63 << 20),
        name="unpack",
    )(a, u, d, g1, g2, vec, out, gt)
    gq, gk, gv, go, gu, gd, gg1, gg2, out, gt = res[:10]
    rn1g, rn1b, rob, rg1b, rn2g, rn2b, rdb, rg2b, rub = [v.reshape(-1) for v in res[10:]]
    return (
        out, gt, rn1g, rn1b, gq, gk, gv, go, rob, gg1, rg1b, rn2g, rn2b, gu, rub, gd, rdb, gg2, rg2b,
    )


def solution(mesh):
    both, rep = P(("dp", "mp"), None), P()
    cols, rows = P(None, "mp"), P("mp", None)
    in_specs = (
        both, P("dp", None), P("dp"), rep, rep, cols, cols, cols, rows, rep, rep, rep, rep, rep, cols,
        P("mp"), rows, rep, rep, rep, both,
    )
    out_specs = (
        both, both, rep, rep, cols, cols, cols, rows, rep, rep, rep, rep, rep, cols, P("mp"), rows, rep,
        rep, rep,
    )
    fn = functools.partial(shards, mesh.shape["dp"])
    return jax.shard_map(fn, mesh=mesh, in_specs=in_specs, out_specs=out_specs, check_vma=False)
```

time: 792 us -> 170 us (0.21); the launches traced: 782 us -> 170 us
  waiting for transfers between devices: 509 us -> 0 us
  Pallas kernels: 0 us -> 169 us
  matrix products: 89.2 us -> 0 us
  local copies, waits for them, and re-layouts: 75.4 us -> 0 us
  blocking collectives: 54.8 us -> 0 us
  other arithmetic: 36.6 us -> 0 us
  between operations: 15.2 us -> 0.83 us
    reduce_scatter x4 -> x0, waiting for transfers between devices: 201 us -> none  [the longest x1 75.7 us: shards(): lax.psum_scatter(jnp.dot(context, output_weight, preferred_element_type=j...]
    pallas_call x0 -> x2, Pallas kernels: none -> 169 us  [the longest x1 164 us: shards(): pl.pallas_call(functools.partial(kernel, ndp, xbits, (*values, *OUT_SHAPE...]
    all_gather x4 -> x0, waiting for transfers between devices: 165 us -> none  [the longest x1 43.5 us: shards(): rows_two = lax.all_gather(rounded_two, 'mp', axis=0, tiled=True)]
    psum x2 -> x0, waiting for transfers between devices: 143 us -> none  [the longest x1 96.4 us: shards(): lax.psum((grad_gate_one_weight, grad_gate_one_bias, grad_output_bias, gra...]
    dot_general x32 -> x0, matrix products: 89.2 us -> none  [the longest x6 21.9 us: contract_cols(): lax.dot_general(left, right, (((1,), (1,)), ((), ())), preferred_element_...]
    psum x2 -> x0, blocking collectives: 54.8 us -> none  [the longest x1 39.9 us: shards(): lax.psum((grad_gate_one_weight, grad_gate_one_bias, grad_output_bias, gra...]
    dynamic_update_slice x8 -> x0, local copies, waits for them, and re-layouts: 42.1 us -> none  [shards(): lax.map(attend_backward, (query, keys, values, doc_ids, logsum, grad_cont...]
    unnamed x125 -> x0, local copies, waits for them, and re-layouts: 13.6 us -> none
  transfers between devices with their start and end apart: 10 -> 0, of which waited for: 10 -> 0; matrix products, arithmetic and copies ran while one was open for 5% -> 0% of each run, Pallas kernels for 0% -> 0%
where the time goes in v1:
time: 170 us
  Pallas kernels  169 us (99%)
    pallas_call x1, Pallas kernels, shards(): pl.pallas_call(functools.partial(kernel, ndp, xbits, (*values, *OUT_SHAPE...  164 us
    pallas_call x1, Pallas kernels, shards(): pl.pallas_call(unpack, out_shape=shapes, in_specs=[vmem] * 8, out_specs=[...  5.19 us

profile of v1, /device:TPU:0, one launch (start us, length us, event | category | flops | bytes accessed | tf_op | source)
XLA Modules:
  0.0 170.0 jit_solution(745338373977406754)
XLA Ops:
  0.7 164.0 %block.1 = (bf16[512,512]{1,0:T(8,128)(2,1)}, f32[512,512]{1,0:T(8,128)}, bf16[8,64,512]{2,1,0:T(8,128)(2,1)}, bf16[8,128,256]{2,1,0:T(8,128)(2,1)}, bf16[8,64,5...) custom-call(bf16[512,512]{1,0:T(8,128)(2,1)} %refs_0_.1, ...), custom_call_target="tpu_custom_call" | custom-call | tf_op jit(solution)/shard_map/block/pallas_call | solution.py:810
  164.6 5.2 %unpack.1 = (f32[512,128]{1,0:T(8,128)}, f32[512,128]{1,0:T(8,128)}, f32[512,128]{1,0:T(8,128)}, f32[128,512]{1,0:T(8,128)}, f32[512,512]{1,0:T(8,128)}, /*index...) custom-call(bf16[8,64,512]{2,1,0:T(8,128)(2,1)} %get-tuple-element.4, ...), custom_call_target="tpu_custom_call" | custom-call | tf_op jit(solution)/shard_map/unpack/pallas_call | solution.py:825

commit v2 on v1

v2 whole, which is shorter than its diff:
```python
import functools
import math
from types import SimpleNamespace

import jax
import jax.numpy as jnp
import numpy as np
from jax import lax
from jax.experimental import pallas as pl
from jax.experimental.pallas import tpu as pltpu
from jax.sharding import PartitionSpec as P

BF = jnp.bfloat16
F32 = jnp.float32
MESH = pl.DeviceIdType.MESH
D = 512
T = 512
S = 1024
HD = 64
CH = 256
NCOPY = 256
GELU_A = math.sqrt(2.0 / math.pi)
GELU_B = 0.044715


def mm(a, b):
    return lax.dot_general(a, b, (((1,), (0,)), ((), ())), preferred_element_type=F32)


def mmt(a, b):
    return lax.dot_general(a, b, (((1,), (1,)), ((), ())), preferred_element_type=F32)


def tmm(a, b):
    return lax.dot_general(a, b, (((0,), (0,)), ((), ())), preferred_element_type=F32)


def sigmoid(v):
    return 0.5 * jnp.tanh(0.5 * v) + 0.5


def colsum(v):
    return jnp.sum(v, axis=0, keepdims=True)


def rowmean(v):
    return jnp.mean(v, axis=-1, keepdims=True)


OUT_SHAPES = dict(
    o_out=((T, D), BF),
    o_gt=((T, D), BF),
    o_a=((8, 64, 512), BF),
    o_u=((8, 128, 256), BF),
    o_d=((8, 64, 512), BF),
    o_g1=((8, 4, 32, 256), BF),
    o_g2=((8, 4, 32, 256), BF),
    o_vec=((16, 512), F32),
)

SCRATCH = dict(
    xt=((T, D), BF), ct=((T, D), BF),
    info=((2, 8, S), F32), dcol=((S, 128), F32), drow=((8, S), F32),
    cttb=((32, S), F32), sttb=((32, S), F32),
    wz=((4, 256, 512), BF), wh=((768, 512), BF), wo=((256, 512), BF),
    upz=((4, 512, 256), BF), dnz=((4, 256, 512), BF), ubz=((4, 8, 256), F32),
    n1=((S, D), BF), xh1=((T, D), F32), rs1=((T, 128), F32), g1=((T, D), F32),
    qt=((4, 64, S), BF), kt=((4, 64, S), BF), vt=((4, 64, S), BF),
    bias=((CH, 2304), F32), pr=((4, CH, 2304), BF), ctxt=((256, S), BF),
    xs=((T, D), BF), xr=((T, D), BF), amx=((T, D), F32), mid=((T, D), F32),
    xh2=((T, D), F32), rs2=((T, 128), F32), n2=((S, D), BF),
    hid=((4, S, 256), BF), gp=((4, S, 256), BF), acc=((T, D), F32), outb=((T, D), BF),
    bl=((S, D), BF), go2=((T, D), BF), gl2=((S, 256), BF),
    al=((S, D), BF), go1=((T, D), BF), gl1=((S, 256), BF), gmr=((T, D), F32),
    dct=((256, S), BF),
    dkt=((64, S), F32), dvt=((64, S), F32), dt=((768, S), BF), gtb=((T, D), BF),
    a_s=((4, 256, 512), BF), a_h=((4, 8, 32, 512), BF), a_b=((4, 64, 512), BF), a_c=((3, 64, 512), BF),
    u_s=((4, 512, 256), BF), u_h=((4, 8, 64, 256), BF), u_b=((4, 128, 256), BF), u_c=((3, 128, 256), BF),
    d_s=((4, 256, 512), BF), d_h=((4, 8, 32, 512), BF), d_b=((4, 64, 512), BF), d_c=((3, 64, 512), BF),
    e_s=((4, 128, 256), BF), e_h=((8, 2, 32, 256), BF), e_b=((4, 32, 256), BF), e_c=((3, 32, 256), BF),
    f_s=((4, 128, 256), BF), f_h=((8, 2, 32, 256), BF), f_b=((4, 32, 256), BF), f_c=((3, 32, 256), BF),
    wg1v=((D, D), BF), wg2v=((D, D), BF),
    pk=((16, 512), F32), pk1=((2, 16, 512), F32), pk2=((4, 16, 512), F32), pk3=((4, 16, 512), F32),
)


def kernel(ndp, xbits, names, *refs):
    R = SimpleNamespace(**dict(zip(names, refs)))
    dp = lax.axis_index("dp")
    m = lax.axis_index("mp")
    bits = [lax.rem(lax.div(dp, 1 << b), 2) for b in range(ndp.bit_length() - 1)]
    c = bits[0]
    g = bits[1] + 2 * bits[2]
    mb = [lax.rem(m, 2), lax.div(m, 2)]

    def flip(value, own, mask):
        for b in range(len(own)):
            if mask >> b & 1:
                value = value + (1 - 2 * own[b]) * (1 << b)
        return value

    dpx = lambda mask: flip(dp, bits, mask)
    mx = lambda mask: flip(m, mb, mask)
    gx = lambda mask: flip(g, bits[1:3], mask)

    def ds(start, size):
        return pl.ds(pl.multiple_of(start, size), size)

    swap = (c + mb[0]) == 1
    r0 = pl.multiple_of(c * T, T)
    p0 = pl.multiple_of(T - c * T, T)
    slot = c * 4 + g
    counter = [0]
    unsent = []

    def remote(src, dst, device, keep=True):
        index = counter[0]
        counter[0] += 1
        copy = pltpu.make_async_remote_copy(
            src_ref=src, dst_ref=dst, send_sem=R.ss.at[index], recv_sem=R.rs.at[index],
            device_id=device, device_id_type=MESH,
        )
        if keep:
            copy.start()
            unsent.append(copy)
        return copy

    def local(src, dst, index):
        return pltpu.make_async_copy(src, dst, R.ls.at[index])

    def arrived(copies):
        for copy in copies:
            copy.wait_recv()

    partner = (dpx(1), m)
    cross = (dpx(1), mx(1))
    chip_x, chip_y = (dpx(2), m), (dpx(4), m)
    near, far = (dp, mx(1)), (dp, mx(3))
    own_rows = pl.ds(r0, T)
    mine_cols = ds(c * 256, 256)
    their_cols = ds(256 - c * 256, 256)

    barrier = pltpu.get_barrier_semaphore()
    friends = [partner, (dpx(2), m), (dpx(4), m), (dpx(6), m)] + [(dp, mx(k)) for k in (1, 2, 3)] + [cross]
    friends += [(dpx(1 << b), m) for b in range(3, 3 + xbits)]
    for friend in friends:
        pl.semaphore_signal(barrier, inc=1, device_id=friend, device_id_type=MESH)
    wz, upz, dnz = R.wz, R.upz, R.dnz
    loads = [
        local(src, dst, 9 + i)
        for i, (src, dst) in enumerate(((R.wg1, R.wg1v), (R.wg2, R.wg2v)))
    ]
    for copy in loads:
        copy.start()
    own_up = local(R.up.at[:, mine_cols], upz.at[m], 0)
    own_dn = local(R.down.at[ds(c * 256, 256), :], dnz.at[m], 1)
    own_up.start()
    own_dn.start()
    loc_x = local(R.tokens, R.xt, 2)
    loc_c = local(R.cot, R.ct, 3)

    @pl.when(jnp.logical_not(swap))
    def _():
        loc_x.start()
        loc_c.start()

    lane = lax.broadcasted_iota(jnp.int32, (64, 128), 1)
    pick = lane == lax.broadcasted_iota(jnp.int32, (64, 128), 0) + c * 64
    pick = jnp.where(pick, 1.0, 0.0).astype(BF)
    wz[m, 0:64, :] = mmt(pick, R.qw[...]).astype(BF)
    wz[m, 64:128, :] = mmt(pick, R.kw[...]).astype(BF)
    wz[m, 128:192, :] = mmt(pick, R.vw[...]).astype(BF)
    wz[m, 192:256, :] = R.ow[ds(c * 64, 64), :]
    ubv = R.ub[...]
    ubv = jnp.where(c == 0, ubv[:, :256], ubv[:, 256:])
    R.ubz[m] = jnp.broadcast_to(ubv, (8, 256))
    info = R.info
    turn = jnp.where(
        lax.broadcasted_iota(jnp.int32, (2, 128), 0) == 0, R.resets[0:1, 0:1], R.resets[0:1, 1:2]
    ).astype(F32)
    info[0] = jnp.zeros((8, S), F32)
    info[0, 0:2, :] = R.docs[...].astype(F32)
    info[0, 2:4, 0:128] = turn

    pl.semaphore_wait(barrier, len(friends))

    swap_x = remote(R.tokens, R.xt, cross, keep=False)
    swap_c = remote(R.cot, R.ct, cross, keep=False)

    near_first = (1, 2, 3)

    def gather(z, rows, lanes):
        quarter = rows // 4
        part = ds(g * quarter, quarter)
        pair = ds(bits[2] * 2 * quarter, 2 * quarter)
        other = ds(gx(2) * quarter, quarter)
        low, high = pl.ds(0, lanes // 2), pl.ds(lanes // 2, lanes // 2)

        def send(block, part, lanes, device):
            return remote(z.at[block, part, lanes], z.at[block, part, lanes], device)

        lines = [send(m, part, pl.ds(0, lanes), (dp, mx(k))) for k in near_first]
        yield
        one, two = [], []
        for k, line in zip(near_first, lines):
            line.wait_recv()
            one.append([send(mx(k), part, low, chip_x), send(mx(k), part, high, chip_y)])
            yield
        for k, copies in zip(near_first, one):
            arrived(copies)
            two.append([
                send(mx(k), pair, low, chip_y), send(mx(k), part, high, chip_x),
                send(mx(k), other, high, chip_x),
            ])
            yield
        for copies in two:
            arrived(copies)
            yield

    def go(steps, count):
        for _ in range(count):
            next(steps)

    get_w, get_u, get_d = gather(wz, 256, 512), gather(upz, 512, 256), gather(dnz, 256, 512)
    next(get_w)

    @pl.when(swap)
    def _():
        swap_x.start()

    own_up.wait()
    next(get_u)
    own_dn.wait()
    next(get_d)

    @pl.when(swap)
    def _():
        swap_c.start()

    send_info = remote(info.at[0], info.at[1], partner)
    ub_copies = [remote(R.ubz.at[m], R.ubz.at[m], (dp, mx(k))) for k in (1, 2, 3)]

    send_info.wait_recv()
    for copy in loads:
        copy.wait()
    row = mb[1]
    mine = jnp.where(swap, 0.0, 1.0)

    def info_row(i):
        return info[0, pl.ds(i, 1), :] * mine + info[1, pl.ds(i, 1), :] * (1.0 - mine)

    doc = info_row(row)
    turn = info_row(row + 2)[:, 0:1]
    R.drow[...] = jnp.broadcast_to(doc, (8, S))
    R.dcol[...] = jnp.broadcast_to(doc, (128, S)).T
    freq = jnp.exp(
        lax.broadcasted_iota(jnp.int32, (32, 1), 0).astype(F32) * (-2.0 * math.log(10000.0) / HD)
    )
    cr, sr = jnp.cos(turn * freq), jnp.sin(turn * freq)
    past = lax.broadcasted_iota(jnp.int32, (1, S), 1).astype(F32) >= turn
    c0, s0 = R.ctab[...], R.stab[...]
    R.cttb[...] = jnp.where(past, c0 * cr + s0 * sr, c0)
    R.sttb[...] = jnp.where(past, s0 * cr - c0 * sr, s0)

    def at(base, i):
        return ds(base + i * CH, CH)

    def chunks(body):
        pl.loop(0, 2)(body)

    go(get_w, 3)

    @pl.when(jnp.logical_not(swap))
    def _():
        loc_x.wait()
        loc_c.wait()

    @pl.when(swap)
    def _():
        swap_x.wait()

    n1 = R.n1

    @chunks
    def _(i):
        rows = at(0, i)
        x = R.xt[rows, :].astype(F32)
        x = x - rowmean(x)
        rstd = lax.rsqrt(rowmean(x * x) + 1e-05)
        xh = x * rstd
        R.xh1[rows, :] = xh
        R.rs1[rows, :] = jnp.broadcast_to(rstd, (CH, 128))
        n1[at(r0, i), :] = (xh * R.n1g[...] + R.n1b[...]).astype(BF)

    send_n1 = remote(n1.at[own_rows, :], n1.at[own_rows, :], partner)
    go(get_w, 3)

    def project(z, base):
        lanes = ds(base, T)
        both = mmt(wz[z, 0:192, :], n1[lanes, :])
        cc, sn = R.cttb[:, lanes], R.sttb[:, lanes]
        for dst, a, b, scale in ((R.qt, both[0:32], both[32:64], 0.125), (R.kt, both[64:96], both[96:128], 1.0)):
            dst[z, 0:32, lanes] = (a * cc - b * sn).astype(BF) * jnp.asarray(scale, BF)
            dst[z, 32:64, lanes] = (b * cc + a * sn).astype(BF) * jnp.asarray(scale, BF)
        R.vt[z, :, lanes] = both[128:192].astype(BF)
        R.wh[ds(z * 192, 192), :] = wz[z, 0:192, :]
        R.wo[ds(z * 64, 64), :] = wz[z, 192:256, :]

    def span(i):
        width = min(i + 1, 3) * CH
        return (i + 1) * CH - width, width

    def lead(i):
        return sum(span(j)[1] for j in range(i))

    def attend(z):
        for i in range(4):
            j0, width = span(i)
            rows, keys = slice(i * CH, (i + 1) * CH), slice(j0, j0 + width)
            here = slice(lead(i), lead(i) + width)
            sc = tmm(R.qt[z, :, rows], R.kt[z, :, keys]) + R.bias[:, here]
            e = jnp.exp(sc - jnp.max(sc, axis=-1, keepdims=True))
            p = (e * (1.0 / jnp.sum(e, axis=-1, keepdims=True))).astype(BF)
            R.pr[z, :, here] = p
            R.ctxt[ds(z * 64, 64), rows] = mmt(R.vt[z, :, keys], p).astype(BF)

    project(m, r0)
    for i in range(4):
        j0, width = span(i)
        dcol = R.dcol[i * CH : (i + 1) * CH, :]
        qi = lax.broadcasted_iota(jnp.int32, (CH, 128), 0) + i * CH
        for w in range(width // 128):
            ki = lax.broadcasted_iota(jnp.int32, (CH, 128), 1) + (j0 + w * 128)
            ok = (dcol == R.drow[0:1, j0 + w * 128 : j0 + w * 128 + 128]) & (ki <= qi)
            R.bias[:, lead(i) + w * 128 : lead(i) + w * 128 + 128] = jnp.where(ok, 0.0, -1e30)
    send_n1.wait_recv()
    go(get_u, 3)
    project(m, p0)
    go(get_d, 3)
    attend(m)

    @chunks
    def _(i):
        gate = mm(n1[at(r0, i), :], R.wg1v[...]) + R.g1b[...]
        R.g1[at(0, i), :] = sigmoid(gate)

    for k in near_first:
        go(get_w, 1)
        project(mx(k), r0)
        project(mx(k), p0)
        if k == 1:
            go(get_u, 3)
        if k == 2:
            go(get_d, 3)
        attend(mx(k))

    def hand_over(body):
        copies = []
        for i in range(2):
            rows = slice(i * CH, i * CH + CH)
            R.xs[rows, :] = body(i).astype(BF)
            copies.append(remote(R.xs.at[rows, :], R.xr.at[rows, :], partner, keep=False))
            copies[i].start()
        return copies

    def wait_all(copies):
        for copy in copies:
            copy.wait()

    send_at = hand_over(lambda i: tmm(R.ctxt[:, at(p0, i)], R.wo[...]))

    @chunks
    def _(i):
        R.amx[at(0, i), :] = tmm(R.ctxt[:, at(r0, i)], R.wo[...])

    wait_all(send_at)
    n2 = R.n2

    @chunks
    def _(i):
        rows = at(0, i)
        x = R.xt[rows, :].astype(F32)
        amx = R.amx[rows, :] + R.xr[rows, :].astype(F32) + R.ob[...] - x
        R.amx[rows, :] = amx
        mid = x + R.g1[rows, :] * amx
        R.mid[rows, :] = mid
        mid = mid - rowmean(mid)
        rstd = lax.rsqrt(rowmean(mid * mid) + 1e-05)
        xh = mid * rstd
        R.xh2[rows, :] = xh
        R.rs2[rows, :] = jnp.broadcast_to(rstd, (CH, 128))
        n2[at(r0, i), :] = (xh * R.n2g[...] + R.n2b[...]).astype(BF)

    send_n2 = remote(n2.at[own_rows, :], n2.at[own_rows, :], partner)
    arrived(ub_copies)

    def up_part(base, z):
        @chunks
        def _(i):
            rows = at(base, i)
            v = mm(n2[rows, :], upz[z]) + R.ubz[z, 0:1, :]
            v2 = v * v
            t = jnp.tanh(GELU_A * v * (1.0 + GELU_B * v2))
            half = 0.5 * (1.0 + t)
            R.hid[z, rows, :] = (v * half).astype(BF)
            slope = half + (0.5 * GELU_A) * v * (1.0 - t * t) * (1.0 + (3.0 * GELU_B) * v2)
            R.gp[z, rows, :] = slope.astype(BF)

    def down_part(base, dst, z, begin):
        @chunks
        def _(i):
            part = mm(R.hid[z, at(base, i), :], dnz[z])
            dst[at(0, i), :] = part if begin else dst[at(0, i), :] + part

    up_part(r0, m)
    send_n2.wait_recv()
    up_part(p0, m)
    for k in near_first:
        go(get_u, 1)
        up_part(r0, mx(k))
        up_part(p0, mx(k))
    down_part(p0, R.acc, m, True)
    down_part(r0, R.gmr, m, True)
    for k in near_first:
        go(get_d, 1)
        down_part(p0, R.acc, mx(k), False)
        if k == near_first[-1]:
            send_br = hand_over(lambda i: R.acc[i * CH : i * CH + CH, :])
        down_part(r0, R.gmr, mx(k), False)

    @pl.when(swap)
    def _():
        swap_c.wait()

    pk = R.pk
    pk[...] = jnp.zeros((16, 512), F32)
    wait_all(send_br)

    @chunks
    def _(i):
        rows = at(0, i)
        gate = sigmoid(mm(n2[at(r0, i), :], R.wg2v[...]) + R.g2b[...])
        mid = R.mid[rows, :]
        bm = R.gmr[rows, :] + R.xr[rows, :].astype(F32) + R.db[...] - mid
        R.outb[rows, :] = (mid + gate * bm).astype(BF)
        cot = R.ct[rows, :].astype(F32)
        gb = gate * cot
        rest = cot - gb
        R.mid[rows, :] = rest
        gg = rest * bm * gate
        R.bl[at(r0, i), :] = gb.astype(BF)
        R.go2[rows, :] = gg.astype(BF)
        pk[6:7, :] += colsum(gb)
        pk[7:8, :] += colsum(gg)

    send_bl = remote(R.bl.at[own_rows, :], R.bl.at[own_rows, :], partner)
    send_gl2 = remote(R.go2.at[:, their_cols], R.gl2.at[own_rows, :], partner)
    keep_gl2 = local(R.go2.at[:, mine_cols], R.gl2.at[own_rows, :], 4)
    keep_gl2.start()
    back_o = remote(R.outb, R.o_out, cross, keep=False)
    keep_o = local(R.outb, R.o_out, 5)

    @pl.when(jnp.logical_not(swap))
    def _():
        keep_o.start()

    def hidden_back(base):
        for z in range(4):
            def step(i, acc, z=z):
                rows = at(base, i)
                gpre = mmt(R.bl[rows, :], dnz[z]) * R.gp[z, rows, :].astype(F32)
                R.gp[z, rows, :] = gpre.astype(BF)
                return acc + colsum(gpre)

            both = lax.fori_loop(0, 2, step, jnp.zeros((1, 256), F32))
            pk[8 + z : 9 + z, 0:256] += jnp.where(c == 0, both, 0.0)
            pk[8 + z : 9 + z, 256:512] += jnp.where(c == 0, 0.0, both)

    def norm_two_part(rows):
        total = mmt(R.gp[0, rows, :], upz[0])
        for z in range(1, 4):
            total = total + mmt(R.gp[z, rows, :], upz[z])
        return total

    def halving(block, buf, dev_a, dev_b, a, b, store):
        f32 = lambda ref: ref[...].astype(F32)
        one = [
            remote(block(a ^ b, 0), buf.at[0], dev_a), remote(block(a ^ b, 1), buf.at[1], dev_b),
            remote(block(a, 0), buf.at[2], dev_a), remote(block(b, 1), buf.at[3], dev_b),
        ]
        yield
        arrived(one[0:2])
        buf[6] = (f32(block(b, 0)) + f32(buf.at[0])).astype(BF)
        buf[7] = (f32(block(a, 1)) + f32(buf.at[1])).astype(BF)
        two = [remote(buf.at[6], buf.at[4], dev_b), remote(buf.at[7], buf.at[5], dev_a)]
        yield
        arrived(one[2:4] + two)
        store(0, (f32(block(0, 0)) + f32(buf.at[2]) + f32(buf.at[4])).astype(BF))
        store(1, (f32(block(0, 1)) + f32(buf.at[3]) + f32(buf.at[5])).astype(BF))

    def exchange(total, buf, dtype):
        for b in range(xbits):
            buf[2 * b] = total.astype(dtype)
            copy = remote(buf.at[2 * b], buf.at[2 * b + 1], (dpx(8 << b), m))
            copy.wait_recv()
            total = buf[2 * b].astype(F32) + buf[2 * b + 1].astype(F32)
        return total

    def chips(out):
        copies = [remote(out.at[slot], out.at[slot], (dpx(2 * k), m)) for k in (1, 2, 3)]
        yield
        arrived(copies)

    def chips_both(out):
        size = out.shape[1] // 2
        low, high = pl.ds(0, size), pl.ds(size, size)
        other = c * 4 + gx(2)
        pair = ds(c * 4 + 2 * bits[2], 2)
        copies = [
            remote(out.at[slot, low], out.at[slot, low], chip_x),
            remote(out.at[slot, high], out.at[slot, high], chip_y),
        ]
        yield
        arrived(copies)
        copies = [
            remote(out.at[pair, low], out.at[pair, low], chip_y),
            remote(out.at[slot, high], out.at[slot, high], chip_x),
            remote(out.at[other, high], out.at[other, high], chip_x),
        ]
        yield
        arrived(copies)

    def cores(out):
        return [remote(out.at[ds(c * 4, 4)], out.at[ds(c * 4, 4)], partner)]

    def finish(out, total, route=chips_both):
        out[slot] = total.astype(BF)
        yield from route(out)
        copies = cores(out)
        yield
        arrived(copies)
        yield

    def finish_all(out, total):
        out[slot, m] = total.astype(BF)
        copies = [remote(out.at[slot, m], out.at[slot, m], (dp, mx(k))) for k in (1, 2, 3)]
        yield
        arrived(copies)
        yield from chips_both(out)
        copies = cores(out)
        yield
        arrived(copies)
        yield

    def over_mp(b_ref, c_ref):
        return [remote(b_ref.at[mx(k)], c_ref.at[k - 1], (dp, mx(k))) for k in (1, 2, 3)]

    def plane_first(s_ref, h_ref, b_ref, c_ref, x_ref, quarter, end, out):
        def block(k, half):
            return s_ref.at[2 * half : 2 * half + 2, ds(gx(k) * quarter, quarter), :]

        def store(half, value):
            b_ref[2 * half : 2 * half + 2] = value

        yield from halving(block, h_ref, chip_x, chip_y, 1, 2, store)
        copies = over_mp(b_ref, c_ref)
        yield True
        arrived(copies)
        total = b_ref[m].astype(F32)
        for k in range(3):
            total = total + c_ref[k].astype(F32)
        yield from end(out, exchange(total, x_ref, BF))

    def block_sum(name, k, quarter, out, route):
        s_ref, h_ref = getattr(R, name + "_s"), getattr(R, name + "_h").at[k]
        b_ref, c_ref = getattr(R, name + "_b"), getattr(R, name + "_c")
        half_rows = quarter // 2

        def block(kk, half):
            return s_ref.at[mx(k), ds(gx(kk) * quarter + half * half_rows, half_rows), :]

        def store(half, value):
            b_ref[k, half * half_rows : half * half_rows + half_rows] = value

        yield from halving(block, h_ref, chip_x, chip_y, 1, 2, store)
        if k:
            waiting.setdefault(name, []).append(remote(b_ref.at[k], c_ref.at[k - 1], (dp, mx(k))))
            return
        yield True
        arrived(waiting[name])
        total = b_ref[0].astype(F32)
        for j in range(3):
            total = total + c_ref[j].astype(F32)
        yield from finish(out, exchange(total, extra(name + "_x"), BF), route)

    waiting, queue, late = {}, [], []

    def begin(steps):
        next(steps)
        queue.append(steps)

    def advance(source):
        steps = source.pop(0)
        for last in steps:
            (late if last or source is late else queue).append(steps)
            break

    def pump(count):
        for _ in range(min(count, len(queue))):
            advance(queue)

    def pump_late(count):
        for _ in range(min(count, len(late))):
            advance(late)

    extra = lambda name: getattr(R, name, None)
    sum_e = plane_first(R.e_s, R.e_h, R.e_b, R.e_c, extra("e_x"), 32, finish_all, R.o_g2)
    sum_f = plane_first(R.f_s, R.f_h, R.f_b, R.f_c, extra("f_x"), 32, finish_all, R.o_g1)
    far_first = (3, 2, 1, 0)

    hidden_back(r0)
    send_bl.wait_recv()
    for k in far_first:
        R.d_s[mx(k)] = tmm(R.hid[mx(k)], R.bl[...]).astype(BF)
        begin(block_sum("d", k, 64, R.o_d, chips_both))
    hidden_back(p0)
    n2t = n2[...].T
    for k in far_first:
        R.u_s[mx(k)] = mm(n2t, R.gp[mx(k)]).astype(BF)
        begin(block_sum("u", k, 128, R.o_u, chips_both))
        pump(1)
    send_gl2.wait_recv()
    keep_gl2.wait()
    full = mm(n2t, R.gl2[...]).astype(BF)
    for z in range(4):
        R.e_s[z] = full[z * 128 : z * 128 + 128, :]
    begin(sum_e)

    send_d2 = hand_over(lambda i: norm_two_part(at(p0, i)))

    @chunks
    def _(i):
        R.gmr[at(0, i), :] = norm_two_part(at(r0, i))

    pump(2)
    wait_all(send_d2)

    @chunks
    def _(i):
        rows = at(0, i)
        gn = R.gmr[rows, :] + R.xr[rows, :].astype(F32) + mmt(R.go2[rows, :], R.wg2v[...])
        xh = R.xh2[rows, :]
        pk[4:5, :] += colsum(gn * xh)
        pk[5:6, :] += colsum(gn)
        e = gn * R.n2g[...]
        gm = R.rs2[rows, 0:1] * (e - rowmean(e) - xh * rowmean(e * xh)) + R.mid[rows, :]
        gate = R.g1[rows, :]
        ga = gate * gm
        gg = (gm - ga) * R.amx[rows, :] * gate
        R.mid[rows, :] = gm - ga
        R.al[at(r0, i), :] = ga.astype(BF)
        R.go1[rows, :] = gg.astype(BF)
        pk[2:3, :] += colsum(ga)
        pk[3:4, :] += colsum(gg)

    send_al = remote(R.al.at[own_rows, :], R.al.at[own_rows, :], partner)
    send_gl1 = remote(R.go1.at[:, their_cols], R.gl1.at[own_rows, :], partner)
    keep_gl1 = local(R.go1.at[:, mine_cols], R.gl1.at[own_rows, :], 6)
    keep_gl1.start()
    n1t = n1[...].T
    send_al.wait_recv()

    @pl.loop(0, 4)
    def _(i):
        rows = at(0, i)
        R.dct[:, rows] = mmt(R.wo[...], R.al[rows, :]).astype(BF)

    pump(3)
    grad_wo = mm(R.ctxt[...], R.al[...]).astype(BF)
    for z in range(4):
        R.a_s[z, 192:256, :] = grad_wo[z * 64 : z * 64 + 64, :]
    send_gl1.wait_recv()
    keep_gl1.wait()
    full = mm(n1t, R.gl1[...]).astype(BF)
    for z in range(4):
        R.f_s[z] = full[z * 128 : z * 128 + 128, :]

    begin(sum_f)
    pump(2)

    @pl.when(swap)
    def _():
        back_o.start()

    dkt, dvt, dt = R.dkt, R.dvt, R.dt

    for k in far_first:
        z = mx(k)
        dkt[...] = jnp.zeros((64, S), F32)
        dvt[...] = jnp.zeros((64, S), F32)
        mine_rows = ds(z * 64, 64)

        def dt_rows(start, size, z=z):
            return pl.ds(pl.multiple_of(z * 192 + start, 32), size)

        for i in range(4):
            j0, width = span(i)
            rows, keys = slice(i * CH, (i + 1) * CH), slice(j0, j0 + width)
            p = R.pr[z, :, lead(i) : lead(i) + width]
            pf = p.astype(F32)
            t = tmm(R.dct[mine_rows, rows], R.vt[z, :, keys]) * pf
            part = (t - pf * jnp.sum(t, axis=-1, keepdims=True)).astype(BF)
            dvt[:, keys] += mm(R.dct[mine_rows, rows], p)
            dkt[:, keys] += mm(R.qt[z, :, rows], part)
            dq = mmt(R.kt[z, :, keys], part) * 0.125
            a, b = dq[0:32], dq[32:64]
            cc, sn = R.cttb[:, rows], R.sttb[:, rows]
            dt[dt_rows(0, 32), rows] = (a * cc + b * sn).astype(BF)
            dt[dt_rows(32, 32), rows] = (b * cc - a * sn).astype(BF)
            pump(1)
            if k == 0:
                pump_late(1)
        a, b = dkt[0:32, :], dkt[32:64, :]
        cc, sn = R.cttb[...], R.sttb[...]
        dt[dt_rows(64, 32), :] = (a * cc + b * sn).astype(BF)
        dt[dt_rows(96, 32), :] = (b * cc - a * sn).astype(BF)
        dt[dt_rows(128, 64), :] = dvt[...].astype(BF)
        R.a_s[z, 0:192, :] = mm(dt[dt_rows(0, 192), :], n1[...]).astype(BF)
        begin(block_sum("a", k, 64, R.o_a, chips))

    send_d1 = hand_over(lambda i: tmm(dt[:, at(p0, i)], R.wh[...]))
    pump(3)

    @chunks
    def _(i):
        R.gmr[at(0, i), :] = tmm(dt[:, at(r0, i)], R.wh[...])

    pump(3)
    wait_all(send_d1)

    def norm_one_back(i):
        rows = slice(i * CH, i * CH + CH)
        gn = R.gmr[rows, :] + R.xr[rows, :].astype(F32) + mmt(R.go1[rows, :], R.wg1v[...])
        xh = R.xh1[rows, :]
        pk[0:1, :] += colsum(gn * xh)
        pk[1:2, :] += colsum(gn)
        e = gn * R.n1g[...]
        grad = R.rs1[rows, 0:1] * (e - rowmean(e) - xh * rowmean(e * xh)) + R.mid[rows, :]
        R.gtb[rows, :] = grad.astype(BF)

    back_t, keep_t = [], []
    for i in range(2):
        norm_one_back(i)
        rows = slice(i * CH, i * CH + CH)
        back_t.append(remote(R.gtb.at[rows, :], R.o_gt.at[rows, :], cross, keep=False))
        keep_t.append(local(R.gtb.at[rows, :], R.o_gt.at[rows, :], 7 + i))

        @pl.when(swap)
        def _():
            back_t[i].start()

        @pl.when(jnp.logical_not(swap))
        def _():
            keep_t[i].start()

    pk1, pk2, pk3 = R.pk1, R.pk2, R.pk3
    pk1[c] = pk[...]
    p_1 = remote(pk1.at[c], pk1.at[c], partner)
    pump(2)
    pump_late(4)
    p_1.wait_recv()
    pk2[g] = pk1[0] + pk1[1]
    p_2 = [remote(pk2.at[g], pk2.at[g], (dpx(2 * k), m)) for k in (1, 2, 3)]
    pump(4)
    pump_late(5)
    arrived(p_2)
    pk3[m] = (pk2[0] + pk2[1]) + (pk2[2] + pk2[3])
    p_3 = [remote(pk3.at[m], pk3.at[m], (dp, mx(k))) for k in (1, 2, 3)]
    pump_late(5)
    arrived(p_3)
    total = exchange((pk3[0] + pk3[1]) + (pk3[2] + pk3[3]), extra("p_x"), F32)
    pk[...] = total
    R.o_vec[...] = total
    R.o_vec[8:9, :] = pk[pl.ds(8 + m, 1), :]
    while late:
        pump_late(1)

    for copy in unsent:
        copy.wait_send()

    @pl.when(swap)
    def _():
        for copy in (back_o, *back_t):
            copy.wait()

    @pl.when(jnp.logical_not(swap))
    def _():
        for copy in (keep_o, *keep_t):
            copy.wait()


def unpack(a, u, d, g1, g2, vec, out, gt, *outs):
    (oq, ok, ov, oo, ou, od, og1, og2, oout, ogt) = outs[:10]
    for j, ref in enumerate((oq, ok, ov)):
        both = jnp.concatenate([a[j].astype(F32), a[4 + j].astype(F32)], axis=0)
        ref[...] = both.T
    for c in range(2):
        oo[c * 64 : c * 64 + 64, :] = a[4 * c + 3].astype(F32)
        for g in range(4):
            ou[g * 128 : g * 128 + 128, c * 256 : c * 256 + 256] = u[4 * c + g].astype(F32)
            od[c * 256 + g * 64 : c * 256 + g * 64 + 64, :] = d[4 * c + g].astype(F32)
            for z in range(4):
                rows = slice(z * 128 + g * 32, z * 128 + g * 32 + 32)
                og1[rows, c * 256 : c * 256 + 256] = g1[4 * c + g, z].astype(F32)
                og2[rows, c * 256 : c * 256 + 256] = g2[4 * c + g, z].astype(F32)
    oout[...] = out[...]
    ogt[...] = gt[...].astype(F32)
    for j, ref in enumerate(outs[10:]):
        ref[...] = vec[j : j + 1, :]


def tables():
    freqs = np.exp(np.arange(HD // 2, dtype=np.float32) * np.float32(-2.0 * math.log(10000.0) / HD))
    angles = np.arange(S, dtype=np.float32)[:, None] * freqs.astype(np.float32)
    angles = angles.T.astype(np.float64)
    return np.cos(angles).astype(np.float32), np.sin(angles).astype(np.float32)


def shards(
    ndp, tokens, doc_ids, resets, n1g, n1b, qw, kw, vw, ow, ob, wg1, g1b, n2g, n2b, up, ub, down, db,
    wg2, g2b, cot,
):
    xbits = ndp.bit_length() - 4
    ctab, stab = tables()
    vector = lambda v: v.reshape(1, -1)
    values = dict(
        tokens=tokens, cot=cot, docs=doc_ids, resets=resets.reshape(1, 2), qw=qw, kw=kw, vw=vw, ow=ow,
        wg1=wg1, up=up, down=down, wg2=wg2, n1g=vector(n1g), n1b=vector(n1b), ob=vector(ob),
        g1b=vector(g1b), n2g=vector(n2g), n2b=vector(n2b), ub=vector(ub), db=vector(db), g2b=vector(g2b),
        ctab=jnp.asarray(ctab), stab=jnp.asarray(stab),
    )
    vmem = pl.BlockSpec(memory_space=pltpu.VMEM)
    anyspace = pl.BlockSpec(memory_space=pl.ANY)
    scratch = {name: pltpu.VMEM(shape, dtype) for name, (shape, dtype) in SCRATCH.items()}
    if xbits:
        more = dict(a_x=(64, 512), u_x=(128, 256), d_x=(64, 512), e_x=(32, 256), f_x=(32, 256))
        for name, shape in more.items():
            scratch[name] = pltpu.VMEM((2 * xbits,) + shape, BF)
        scratch.update(p_x=pltpu.VMEM((2 * xbits, 16, 512), F32))
    copies = pltpu.SemaphoreType.DMA((NCOPY + 6 * xbits,))
    scratch.update(
        ss=copies, rs=copies, ls=pltpu.SemaphoreType.DMA((13,))
    )
    in_specs = dict.fromkeys(values, vmem)
    in_specs.update(tokens=anyspace, cot=anyspace, up=anyspace, down=anyspace)
    in_specs.update(wg1=anyspace, wg2=anyspace)
    packed = pl.pallas_call(
        functools.partial(kernel, ndp, xbits, (*values, *OUT_SHAPES, *scratch)),
        out_shape=[jax.ShapeDtypeStruct(shape, dtype) for shape, dtype in OUT_SHAPES.values()],
        in_specs=list(in_specs.values()),
        out_specs=[vmem] * len(OUT_SHAPES),
        scratch_shapes=list(scratch.values()),
        compiler_params=pltpu.CompilerParams(
            collective_id=0, has_side_effects=True, vmem_limit_bytes=64 << 20
        ),
        name="block",
    )(*values.values())
    out, gt, a, u, d, g1, g2, vec = packed
    f32 = lambda *shape: jax.ShapeDtypeStruct(shape, F32)
    shapes = [f32(D, 128)] * 3 + [f32(128, D)] + [f32(D, D)] * 4
    shapes += [jax.ShapeDtypeStruct((T, D), BF), f32(T, D)] + [f32(1, D)] * 9
    res = pl.pallas_call(
        unpack,
        out_shape=shapes,
        in_specs=[vmem] * 8,
        out_specs=[vmem] * len(shapes),
        compiler_params=pltpu.CompilerParams(vmem_limit_bytes=63 << 20),
        name="unpack",
    )(a, u, d, g1, g2, vec, out, gt)
    gq, gk, gv, go, gu, gd, gg1, gg2, out, gt = res[:10]
    rn1g, rn1b, rob, rg1b, rn2g, rn2b, rdb, rg2b, rub = [v.reshape(-1) for v in res[10:]]
    return (
        out, gt, rn1g, rn1b, gq, gk, gv, go, rob, gg1, rg1b, rn2g, rn2b, gu, rub, gd, rdb, gg2, rg2b,
    )


def solution(mesh):
    both, rep = P(("dp", "mp"), None), P()
    cols, rows = P(None, "mp"), P("mp", None)
    in_specs = (
        both, P("dp", None), P("dp"), rep, rep, cols, cols, cols, rows, rep, rep, rep, rep, rep, cols,
        P("mp"), rows, rep, rep, rep, both,
    )
    out_specs = (
        both, both, rep, rep, cols, cols, cols, rows, rep, rep, rep, rep, rep, cols, P("mp"), rows, rep,
        rep, rep,
    )
    fn = functools.partial(shards, mesh.shape["dp"])
    return jax.shard_map(fn, mesh=mesh, in_specs=in_specs, out_specs=out_specs, check_vma=False)
```

time: 170 us -> 125 us (0.74)
  Pallas kernels: 169 us -> 124 us
    pallas_call x1, Pallas kernels: 164 us -> 119 us  [shards(): pl.pallas_call(functools.partial(kernel, ndp, xbits, (*values, *OUT_SHAPE...]
where the time goes in v2:
time: 125 us
  Pallas kernels  124 us (99%)
    pallas_call x1, Pallas kernels, shards(): pl.pallas_call(functools.partial(kernel, ndp, xbits, (*values, *OUT_SHAPE...  119 us
    pallas_call x1, Pallas kernels, shards(): pl.pallas_call(unpack, out_shape=shapes, in_specs=[vmem] * 8, out_specs=[...  5.02 us

profile of v2, /device:TPU:0, one launch (start us, length us, event | category | flops | bytes accessed | tf_op | source)
XLA Modules:
  0.0 125.1 jit_solution(18141738716521102097)
XLA Ops:
  0.7 119.3 %block.1 = (bf16[512,512]{1,0:T(8,128)(2,1)}, bf16[512,512]{1,0:T(8,128)(2,1)}, bf16[8,64,512]{2,1,0:T(8,128)(2,1)}, bf16[8,128,256]{2,1,0:T(8,128)(2,1)}, bf16[...) custom-call(bf16[512,512]{1,0:T(8,128)(2,1)} %refs_0_.1, ...), custom_call_target="tpu_custom_call" | custom-call | tf_op jit(solution)/shard_map/block/pallas_call | solution.py:857
  120.0 5.0 %unpack.1 = (f32[512,128]{1,0:T(8,128)}, f32[512,128]{1,0:T(8,128)}, f32[512,128]{1,0:T(8,128)}, f32[128,512]{1,0:T(8,128)}, f32[512,512]{1,0:T(8,128)}, /*index...) custom-call(bf16[8,64,512]{2,1,0:T(8,128)(2,1)} %get-tuple-element.4, ...), custom_call_target="tpu_custom_call" | custom-call | tf_op jit(solution)/shard_map/unpack/pallas_call | solution.py:872

commit v3 on v2

--- a/solution.py
+++ b/solution.py
@@ -19,6 +19,8 @@
 HD = 64
 CH = 256
 NCOPY = 256
+IN = "in_"
+BIG = ("tokens", "cot", "up", "down", "wg1", "wg2")
 GELU_A = math.sqrt(2.0 / math.pi)
 GELU_B = 0.044715
 
@@ -80,6 +82,8 @@
     e_s=((4, 128, 256), BF), e_h=((8, 2, 32, 256), BF), e_b=((4, 32, 256), BF), e_c=((3, 32, 256), BF),
     f_s=((4, 128, 256), BF), f_h=((8, 2, 32, 256), BF), f_b=((4, 32, 256), BF), f_c=((3, 32, 256), BF),
     wg1v=((D, D), BF), wg2v=((D, D), BF),
+    p_a=((8, 64, 512), BF), p_u=((8, 128, 256), BF), p_d=((8, 64, 512), BF),
+    p_g1=((8, 4, 32, 256), BF), p_g2=((8, 4, 32, 256), BF), p_vec=((16, 512), F32),
     pk=((16, 512), F32), pk1=((2, 16, 512), F32), pk2=((4, 16, 512), F32), pk3=((4, 16, 512), F32),
 )
 
@@ -152,6 +156,14 @@
     ]
     for copy in loads:
         copy.start()
+    small = [name for name in names if hasattr(R, IN + name)]
+    enter = [
+        pltpu.make_async_copy(getattr(R, name), getattr(R, IN + name), R.ins.at[i])
+        for i, name in enumerate(small)
+    ]
+    for name, copy in zip(small, enter):
+        copy.start()
+        setattr(R, name, getattr(R, IN + name))
     own_up = local(R.up.at[:, mine_cols], upz.at[m], 0)
     own_dn = local(R.down.at[ds(c * 256, 256), :], dnz.at[m], 1)
     own_up.start()
@@ -163,6 +175,9 @@
     def _():
         loc_x.start()
         loc_c.start()
+
+    for copy in enter:
+        copy.wait()
 
     lane = lax.broadcasted_iota(jnp.int32, (64, 128), 1)
     pick = lane == lax.broadcasted_iota(jnp.int32, (64, 128), 0) + c * 64
@@ -400,10 +415,10 @@
             rows = at(base, i)
             v = mm(n2[rows, :], upz[z]) + R.ubz[z, 0:1, :]
             v2 = v * v
-            t = jnp.tanh(GELU_A * v * (1.0 + GELU_B * v2))
-            half = 0.5 * (1.0 + t)
-            R.hid[z, rows, :] = (v * half).astype(BF)
-            slope = half + (0.5 * GELU_A) * v * (1.0 - t * t) * (1.0 + (3.0 * GELU_B) * v2)
+            half = 0.5 * jnp.tanh(v * (GELU_A + (GELU_A * GELU_B) * v2)) + 0.5
+            hid = v * half
+            R.hid[z, rows, :] = hid.astype(BF)
+            slope = half + hid * (1.0 - half) * (2.0 * GELU_A + (6.0 * GELU_A * GELU_B) * v2)
             R.gp[z, rows, :] = slope.astype(BF)
 
     def down_part(base, dst, z, begin):
@@ -533,13 +548,24 @@
     def cores(out):
         return [remote(out.at[ds(c * 4, 4)], out.at[ds(c * 4, 4)], partner)]
 
+    def flush(buf):
+        copy = local(buf, homes[id(buf)], 12 + len(flushed))
+        copy.start()
+        flushed.append(copy)
+
+    flushed = []
+    homes = {
+        id(R.p_a): R.o_a, id(R.p_u): R.o_u, id(R.p_d): R.o_d, id(R.p_g1): R.o_g1, id(R.p_g2): R.o_g2,
+        id(R.p_vec): R.o_vec,
+    }
+
     def finish(out, total, route=chips_both):
         out[slot] = total.astype(BF)
         yield from route(out)
         copies = cores(out)
         yield
         arrived(copies)
-        yield
+        flush(out)
 
     def finish_all(out, total):
         out[slot, m] = total.astype(BF)
@@ -550,7 +576,7 @@
         copies = cores(out)
         yield
         arrived(copies)
-        yield
+        flush(out)
 
     def over_mp(b_ref, c_ref):
         return [remote(b_ref.at[mx(k)], c_ref.at[k - 1], (dp, mx(k))) for k in (1, 2, 3)]
@@ -582,7 +608,23 @@
         def store(half, value):
             b_ref[k, half * half_rows : half * half_rows + half_rows] = value
 
-        yield from halving(block, h_ref, chip_x, chip_y, 1, 2, store)
+        def direct():
+            copies = [
+                remote(block(kk, half), h_ref.at[2 * kk - 2 + half], (dpx(2 * kk), m))
+                for kk in (1, 2, 3) for half in (0, 1)
+            ]
+            yield
+            arrived(copies)
+            for half in (0, 1):
+                total = block(0, half)[...].astype(F32)
+                for kk in (1, 2, 3):
+                    total = total + h_ref[2 * kk - 2 + half].astype(F32)
+                store(half, total.astype(BF))
+
+        if name == "a" and k == 0:
+            yield from direct()
+        else:
+            yield from halving(block, h_ref, chip_x, chip_y, 1, 2, store)
         if k:
             waiting.setdefault(name, []).append(remote(b_ref.at[k], c_ref.at[k - 1], (dp, mx(k))))
             return
@@ -614,20 +656,20 @@
             advance(late)
 
     extra = lambda name: getattr(R, name, None)
-    sum_e = plane_first(R.e_s, R.e_h, R.e_b, R.e_c, extra("e_x"), 32, finish_all, R.o_g2)
-    sum_f = plane_first(R.f_s, R.f_h, R.f_b, R.f_c, extra("f_x"), 32, finish_all, R.o_g1)
+    sum_e = plane_first(R.e_s, R.e_h, R.e_b, R.e_c, extra("e_x"), 32, finish_all, R.p_g2)
+    sum_f = plane_first(R.f_s, R.f_h, R.f_b, R.f_c, extra("f_x"), 32, finish_all, R.p_g1)
     far_first = (3, 2, 1, 0)
 
     hidden_back(r0)
     send_bl.wait_recv()
     for k in far_first:
         R.d_s[mx(k)] = tmm(R.hid[mx(k)], R.bl[...]).astype(BF)
-        begin(block_sum("d", k, 64, R.o_d, chips_both))
+        begin(block_sum("d", k, 64, R.p_d, chips_both))
     hidden_back(p0)
     n2t = n2[...].T
     for k in far_first:
         R.u_s[mx(k)] = mm(n2t, R.gp[mx(k)]).astype(BF)
-        begin(block_sum("u", k, 128, R.o_u, chips_both))
+        begin(block_sum("u", k, 128, R.p_u, chips_both))
         pump(1)
     send_gl2.wait_recv()
     keep_gl2.wait()
@@ -717,7 +759,8 @@
             cc, sn = R.cttb[:, rows], R.sttb[:, rows]
             dt[dt_rows(0, 32), rows] = (a * cc + b * sn).astype(BF)
             dt[dt_rows(32, 32), rows] = (b * cc - a * sn).astype(BF)
-            pump(1)
+            if i >= 4 - (4, 3, 3, 2)[3 - k]:
+                pump(1)
             if k == 0:
                 pump_late(1)
         a, b = dkt[0:32, :], dkt[32:64, :]
@@ -726,7 +769,7 @@
         dt[dt_rows(96, 32), :] = (b * cc - a * sn).astype(BF)
         dt[dt_rows(128, 64), :] = dvt[...].astype(BF)
         R.a_s[z, 0:192, :] = mm(dt[dt_rows(0, 192), :], n1[...]).astype(BF)
-        begin(block_sum("a", k, 64, R.o_a, chips))
+        begin(block_sum("a", k, 64, R.p_a, chips))
 
     send_d1 = hand_over(lambda i: tmm(dt[:, at(p0, i)], R.wh[...]))
     pump(3)
@@ -780,13 +823,17 @@
     arrived(p_3)
     total = exchange((pk3[0] + pk3[1]) + (pk3[2] + pk3[3]), extra("p_x"), F32)
     pk[...] = total
-    R.o_vec[...] = total
-    R.o_vec[8:9, :] = pk[pl.ds(8 + m, 1), :]
-    while late:
+    R.p_vec[...] = total
+    R.p_vec[8:9, :] = pk[pl.ds(8 + m, 1), :]
+    flush(R.p_vec)
+    while queue or late:
+        pump(1)
         pump_late(1)
 
     for copy in unsent:
         copy.wait_send()
+    for copy in flushed:
+        copy.wait()
 
     @pl.when(swap)
     def _():
@@ -849,16 +896,18 @@
         scratch.update(p_x=pltpu.VMEM((2 * xbits, 16, 512), F32))
     copies = pltpu.SemaphoreType.DMA((NCOPY + 6 * xbits,))
     scratch.update(
-        ss=copies, rs=copies, ls=pltpu.SemaphoreType.DMA((13,))
+        ss=copies, rs=copies, ls=pltpu.SemaphoreType.DMA((20,))
     )
-    in_specs = dict.fromkeys(values, vmem)
-    in_specs.update(tokens=anyspace, cot=anyspace, up=anyspace, down=anyspace)
-    in_specs.update(wg1=anyspace, wg2=anyspace)
+    in_specs = dict.fromkeys(values, anyspace)
+    small = [name for name in values if name not in BIG]
+    for name in small:
+        scratch[IN + name] = pltpu.VMEM(values[name].shape, values[name].dtype)
+    scratch.update(ins=pltpu.SemaphoreType.DMA((len(small),)))
     packed = pl.pallas_call(
         functools.partial(kernel, ndp, xbits, (*values, *OUT_SHAPES, *scratch)),
         out_shape=[jax.ShapeDtypeStruct(shape, dtype) for shape, dtype in OUT_SHAPES.values()],
         in_specs=list(in_specs.values()),
-        out_specs=[vmem] * len(OUT_SHAPES),
+        out_specs=[anyspace] * len(OUT_SHAPES),
         scratch_shapes=list(scratch.values()),
         compiler_params=pltpu.CompilerParams(
             collective_id=0, has_side_effects=True, vmem_limit_bytes=64 << 20

time: 125 us -> 120 us (0.960)
  Pallas kernels: 124 us -> 119 us
    pallas_call x1, Pallas kernels: 119 us -> 114 us  [shards(): pl.pallas_call(functools.partial(kernel, ndp, xbits, (*values, *OUT_SHAPE...]
where the time goes in v3:
time: 120 us
  Pallas kernels  119 us (99%)
    pallas_call x1, Pallas kernels, shards(): pl.pallas_call(functools.partial(kernel, ndp, xbits, (*values, *OUT_SHAPE...  114 us
    pallas_call x1, Pallas kernels, shards(): pl.pallas_call(unpack, out_shape=shapes, in_specs=[vmem] * 8, out_specs=[...  5.02 us

profile of v3, /device:TPU:0, one launch (start us, length us, event | category | flops | bytes accessed | tf_op | source)
XLA Modules:
  0.0 119.5 jit_solution(8441197238650261854)
XLA Ops:
  0.7 113.6 %block.1 = (bf16[512,512]{1,0:T(8,128)(2,1)}, bf16[512,512]{1,0:T(8,128)(2,1)}, bf16[8,64,512]{2,1,0:T(8,128)(2,1)}, bf16[8,128,256]{2,1,0:T(8,128)(2,1)}, bf16[...) custom-call(bf16[512,512]{1,0:T(8,128)(2,1)} %refs_0_.1, ...), custom_call_target="tpu_custom_call" | custom-call | tf_op jit(solution)/shard_map/block/pallas_call | solution.py:906
  114.3 5.0 %unpack.1 = (f32[512,128]{1,0:T(8,128)}, f32[512,128]{1,0:T(8,128)}, f32[512,128]{1,0:T(8,128)}, f32[128,512]{1,0:T(8,128)}, f32[512,512]{1,0:T(8,128)}, /*index...) custom-call(bf16[8,64,512]{2,1,0:T(8,128)(2,1)} %get-tuple-element.4, ...), custom_call_target="tpu_custom_call" | custom-call | tf_op jit(solution)/shard_map/unpack/pallas_call | solution.py:921

commit v4 on v3

--- a/solution.py
+++ b/solution.py
@@ -351,8 +351,8 @@
     send_n1.wait_recv()
     go(get_u, 3)
     project(m, p0)
+    attend(m)
     go(get_d, 3)
-    attend(m)
 
     @chunks
     def _(i):
@@ -474,6 +474,10 @@
     keep_gl2.start()
     back_o = remote(R.outb, R.o_out, cross, keep=False)
     keep_o = local(R.outb, R.o_out, 5)
+
+    @pl.when(swap)
+    def _():
+        back_o.start()
 
     @pl.when(jnp.logical_not(swap))
     def _():
@@ -729,10 +733,6 @@
 
     begin(sum_f)
     pump(2)
-
-    @pl.when(swap)
-    def _():
-        back_o.start()
 
     dkt, dvt, dt = R.dkt, R.dvt, R.dt
 

time: 120 us -> 118 us (0.983)
  Pallas kernels: 119 us -> 117 us
    pallas_call x1, Pallas kernels: 114 us -> 112 us  [shards(): pl.pallas_call(functools.partial(kernel, ndp, xbits, (*values, *OUT_SHAPE...]
where the time goes in v4:
time: 118 us
  Pallas kernels  117 us (99%)
    pallas_call x1, Pallas kernels, shards(): pl.pallas_call(functools.partial(kernel, ndp, xbits, (*values, *OUT_SHAPE...  112 us
    pallas_call x1, Pallas kernels, shards(): pl.pallas_call(unpack, out_shape=shapes, in_specs=[vmem] * 8, out_specs=[...  5.02 us

profile of v4, /device:TPU:0, one launch (start us, length us, event | category | flops | bytes accessed | tf_op | source)
XLA Modules:
  0.0 117.7 jit_solution(9300406495616887014)
XLA Ops:
  0.7 111.9 %block.1 = (bf16[512,512]{1,0:T(8,128)(2,1)}, bf16[512,512]{1,0:T(8,128)(2,1)}, bf16[8,64,512]{2,1,0:T(8,128)(2,1)}, bf16[8,128,256]{2,1,0:T(8,128)(2,1)}, bf16[...) custom-call(bf16[512,512]{1,0:T(8,128)(2,1)} %refs_0_.1, ...), custom_call_target="tpu_custom_call" | custom-call | tf_op jit(solution)/shard_map/block/pallas_call | solution.py:906
  112.6 5.0 %unpack.1 = (f32[512,128]{1,0:T(8,128)}, f32[512,128]{1,0:T(8,128)}, f32[512,128]{1,0:T(8,128)}, f32[128,512]{1,0:T(8,128)}, f32[512,512]{1,0:T(8,128)}, /*index...) custom-call(bf16[8,64,512]{2,1,0:T(8,128)(2,1)} %get-tuple-element.4, ...), custom_call_target="tpu_custom_call" | custom-call | tf_op jit(solution)/shard_map/unpack/pallas_call | solution.py:921

commit v5 on v4

--- a/solution.py
+++ b/solution.py
@@ -248,10 +248,6 @@
     own_dn.wait()
     next(get_d)
 
-    @pl.when(swap)
-    def _():
-        swap_c.start()
-
     send_info = remote(info.at[0], info.at[1], partner)
     ub_copies = [remote(R.ubz.at[m], R.ubz.at[m], (dp, mx(k))) for k in (1, 2, 3)]
 
@@ -353,6 +349,11 @@
     project(m, p0)
     attend(m)
     go(get_d, 3)
+
+    @pl.when(swap)
+    def _():
+        swap_c.start()
+
 
     @chunks
     def _(i):

time: 118 us -> 118 us (level)
  no operation moved by 1% of the time
where the time goes in v5:
time: 118 us
  Pallas kernels  117 us (99%)
    pallas_call x1, Pallas kernels, shards(): pl.pallas_call(functools.partial(kernel, ndp, xbits, (*values, *OUT_SHAPE...  112 us
    pallas_call x1, Pallas kernels, shards(): pl.pallas_call(unpack, out_shape=shapes, in_specs=[vmem] * 8, out_specs=[...  5.02 us

profile of v5, /device:TPU:0, one launch (start us, length us, event | category | flops | bytes accessed | tf_op | source)
XLA Modules:
  0.0 117.7 jit_solution(8969202237562149852)
XLA Ops:
  0.7 111.9 %block.1 = (bf16[512,512]{1,0:T(8,128)(2,1)}, bf16[512,512]{1,0:T(8,128)(2,1)}, bf16[8,64,512]{2,1,0:T(8,128)(2,1)}, bf16[8,128,256]{2,1,0:T(8,128)(2,1)}, bf16[...) custom-call(bf16[512,512]{1,0:T(8,128)(2,1)} %refs_0_.1, ...), custom_call_target="tpu_custom_call" | custom-call | tf_op jit(solution)/shard_map/block/pallas_call | solution.py:907
  112.6 5.0 %unpack.1 = (f32[512,128]{1,0:T(8,128)}, f32[512,128]{1,0:T(8,128)}, f32[512,128]{1,0:T(8,128)}, f32[128,512]{1,0:T(8,128)}, f32[512,512]{1,0:T(8,128)}, /*index...) custom-call(bf16[8,64,512]{2,1,0:T(8,128)(2,1)} %get-tuple-element.4, ...), custom_call_target="tpu_custom_call" | custom-call | tf_op jit(solution)/shard_map/unpack/pallas_call | solution.py:922
